TPU v7x, 32 devices: a whole 2x2x4 slice. The times are simulated.
32 devices in a mesh: leaf: 8 (over z, y), sep: 4 (over x, core).
Axes of the slice: x: 2, y: 2, z: 4, core: 2. Of those that a mesh axis runs over, the one named last changes fastest.
Arguments:
- leaf_rhs: float32 [12288, 128], P(('leaf', 'sep')), may hold values from -6 to 6
- leaf_inverse: float32 [12288, 64], P(('leaf', 'sep')), may hold values from -1 to 1
- leaf_coupling: bfloat16 [2, 8192, 12288], P(None, None, ('leaf', 'sep')), may hold values from -0.21875 to 0.21875
- tile_mask: int32 [2, 128, 192], P(None, None, ('leaf', 'sep')), may hold values 0 or 1
- low_rhs: float32 [16384, 128], P(('leaf', 'sep')), may hold values from -6 to 6
- top_rhs: float32 [8192, 128], P(('leaf', 'sep')), may hold values from -6 to 6
- low_inverse: float32 [16384, 8192], P(('leaf', 'sep')), may hold values from -0.0625 to 0.0625
- top_inverse: float32 [8192, 8192], P(('leaf', 'sep')), may hold values from -0.0625 to 0.0625
- low_coupling: float32 [8192, 16384], P(None, ('leaf', 'sep')), may hold values from -0.0625 to 0.0625
Outputs:
- interior_solution: float32 [12288, 128], P(('leaf', 'sep'))
- top_solution: float32 [8192, 128], P(('leaf', 'sep'))
All inputs are finite; a program needn't handle non-finite values. No bound on the sum of `tile_mask` on one device may be relied on, other than what follows from the above.
Results may differ from a plain program's by a relative error of at most 0.0033.
Values may be sent and summed in bfloat16 or wider, within the bound.
No kernel may reach another device: no remote copies, remote signals or barrier semaphores. Data moves between devices by JAX's collectives and lax.ppermute only.
A program may use at most 192 MiB of HBM per device.

v0:
```python
import jax
import jax.numpy as jnp
from jax import lax
from jax.sharding import PartitionSpec as P

PRECISE = lax.Precision.HIGHEST


def swapped(block, axis, stride):
    count = lax.axis_size(axis)
    route = []
    for low in range(count):
        high = low | 1 << stride
        if high != low and high < count:
            route += [(low, high), (high, low)]
    return lax.ppermute(block, axis, route)


def lower_mask(block_size):
    row_index = lax.broadcasted_iota(jnp.int32, (block_size, block_size), 0)
    column_index = lax.broadcasted_iota(jnp.int32, (block_size, block_size), 1)
    return (row_index >= column_index).astype(jnp.float32)


def band_mask(row_start, row_count, column_count):
    row_index = lax.broadcasted_iota(jnp.int32, (row_count, column_count), 0) + row_start
    column_index = lax.broadcasted_iota(jnp.int32, (row_count, column_count), 1)
    return (row_index >= column_index).astype(jnp.float32)


def tree_sum(partial_value, leaf_bits, rounded):
    sep_bits = lax.axis_size("sep").bit_length() - 1
    leaf_index = lax.axis_index("leaf")
    sep_index = lax.axis_index("sep")
    step_list = [("sep", bit_number) for bit_number in range(sep_bits)] + [
        ("leaf", bit_number) for bit_number in range(leaf_bits)
    ]
    columns = partial_value.shape[1]
    for axis_name, bit_number in step_list:
        owner_index = sep_index if axis_name == "sep" else leaf_index
        chosen = owner_index >> bit_number & 1
        halves = partial_value.reshape(2, partial_value.shape[0] // 2, columns)
        retained = lax.dynamic_index_in_dim(halves, chosen, 0, keepdims=False)
        outgoing = lax.dynamic_index_in_dim(halves, 1 - chosen, 0, keepdims=False)
        if axis_name == "sep":
            received = swapped(outgoing, "sep", bit_number)
        else:
            received = swapped(outgoing, "leaf", bit_number)
        partial_value = retained + received
    if rounded:
        partial_value = partial_value.astype(jnp.bfloat16)
    for axis_name, bit_number in reversed(step_list):
        owner_index = sep_index if axis_name == "sep" else leaf_index
        chosen = owner_index >> bit_number & 1
        if rounded:
            if axis_name == "sep":
                partner = swapped(partial_value, "sep", bit_number)
            else:
                partner = swapped(partial_value, "leaf", bit_number)
        elif axis_name == "sep":
            partner = swapped(partial_value, "sep", bit_number)
        else:
            partner = swapped(partial_value, "leaf", bit_number)
        partial_value = jnp.where(
            chosen == 0,
            jnp.concatenate([partial_value, partner], 0),
            jnp.concatenate([partner, partial_value], 0),
        )
    return partial_value


def top_total(partial_value):
    return lax.psum(partial_value, ("leaf", "sep"))


def body(
    leaf_rhs,
    leaf_inverse,
    leaf_coupling,
    tile_mask,
    low_rhs,
    top_rhs,
    low_inverse,
    top_inverse,
    low_coupling,
):
    leaf_count = lax.axis_size("leaf")
    sep_count = lax.axis_size("sep")
    device_total = leaf_count * sep_count
    leaf_bits = leaf_count.bit_length() - 1
    device_place = lax.axis_index("leaf") * sep_count + lax.axis_index("sep")
    local_rows = leaf_rhs.shape[0]
    columns = leaf_rhs.shape[1]
    block_size = leaf_inverse.shape[1]
    sep_size = low_inverse.shape[1]
    level_total = leaf_coupling.shape[0]
    triangle = lower_mask(block_size)
    inverses = leaf_inverse.reshape(local_rows // block_size, block_size, block_size) * triangle
    forward_leaf = jnp.einsum(
        "nij,njc->nic",
        inverses,
        leaf_rhs.reshape(local_rows // block_size, block_size, columns),
        precision=PRECISE,
    ).reshape(local_rows, columns)
    rounded_leaf = forward_leaf.astype(jnp.bfloat16)
    spread = tile_mask.astype(jnp.bfloat16)[:, :, None, :, None]
    masked = (
        leaf_coupling.reshape(
            level_total, tile_mask.shape[1], block_size, local_rows // block_size, block_size
        )
        * spread
    ).reshape(level_total, sep_size, local_rows)
    partial_value = jnp.einsum(
        "tsr,rc->tsc", masked, rounded_leaf, preferred_element_type=jnp.float32
    )
    low_count = low_inverse.shape[0]
    low_start = device_place % (device_total // 2) * low_count
    top_count = top_inverse.shape[0]
    top_start = device_place * top_count
    low_factor = low_inverse * band_mask(low_start, low_count, sep_size)
    top_factor = top_inverse * band_mask(top_start, top_count, sep_size)
    blank = jnp.zeros((sep_size, columns), jnp.float32)
    low_gap = lax.dynamic_update_slice_in_dim(blank, low_rhs, low_start, 0) - partial_value[0]
    first_input = tree_sum(low_gap, leaf_bits - 1, False)
    first_rows = jnp.dot(low_factor, first_input, precision=PRECISE)
    top_gap = (
        lax.dynamic_update_slice_in_dim(blank, top_rhs, top_start, 0)
        - partial_value[1]
        - jnp.dot(low_coupling, first_rows, precision=PRECISE)
    )
    top_input = top_total(top_gap)
    forward_rows = jnp.dot(top_factor, top_input, precision=PRECISE)
    top_solution = top_total(jnp.dot(top_factor.T, forward_rows, precision=PRECISE))
    carried = jnp.dot(low_coupling.T, top_solution, precision=PRECISE)
    back_rounded = tree_sum(
        jnp.dot(low_factor.T, first_rows - carried, precision=PRECISE), leaf_bits - 1, True
    )
    top_rounded = top_solution.astype(jnp.bfloat16)
    path_rounded = jnp.stack([back_rounded, top_rounded])
    leaf_back = jnp.einsum("tsr,tsc->rc", masked, path_rounded, preferred_element_type=jnp.float32)
    interior_solution = jnp.einsum(
        "nji,njc->nic",
        inverses,
        (forward_leaf - leaf_back).reshape(local_rows // block_size, block_size, columns),
        precision=PRECISE,
    ).reshape(local_rows, columns)
    return (interior_solution, lax.dynamic_slice_in_dim(top_solution, top_start, top_count, 0))


def solution(mesh):
    return jax.shard_map(
        body,
        mesh=mesh,
        in_specs=(
            P(("leaf", "sep"), None),
            P(("leaf", "sep"), None),
            P(None, None, ("leaf", "sep")),
            P(None, None, ("leaf", "sep")),
            P(("leaf", "sep"), None),
            P(("leaf", "sep"), None),
            P(("leaf", "sep"), None),
            P(("leaf", "sep"), None),
            P(None, ("leaf", "sep")),
        ),
        out_specs=(P(("leaf", "sep"), None), P(("leaf", "sep"), None)),
        check_vma=False,
    )
```

profile of v0, /device:TPU:25, one launch (start us, length us, event | category | flops | bytes accessed | tf_op | source)
XLA Modules:
  0.0 685.7 jit_solution(14286367782686833670)
XLA Ops:
  10.2 9.1 %mul.36 = bf16[2,128,64,6,64]{2,1,4,3,0:T(8,128)(2,1)} broadcast(bf16[2,128,6]{1,2,0:T(8,128)(2,1)S(1)} %copy.16), dimensions={0,1,3} | broadcast | bytes 12585984 | tf_op jit(solution)/shard_map/mul | solution.py:108
  19.4 32.8 %mul.37 = bf16[2,8192,384]{1,2,0:T(8,128)(2,1)} reshape(bf16[2,128,64,6,64]{2,1,4,3,0:T(8,128)(2,1)} %mul.36) | data formatting | bytes 25165824 | tf_op jit(solution)/shard_map/mul | solution.py:108
  52.2 16.7 %copy.17 = bf16[2,8192,384]{1,2,0:T(8,128)(2,1)} copy(bf16[2,8192,384]{2,1,0:T(8,128)(2,1)} %param.11) | data formatting | bytes 25165824 | tf_op args[2]
  68.9 9.9 %mul.38 = bf16[2,8192,384]{1,2,0:T(8,128)(2,1)S(1)} multiply(bf16[2,8192,384]{1,2,0:T(8,128)(2,1)} %copy.17, bf16[2,8192,384]{1,2,0:T(8,128)(2,1)} %mul.37) | non-fusion elementwise | flops 6291456 | bytes 37748736 | tf_op jit(solution)/shard_map/mul | solution.py:108
  78.8 3.5 fusion.43
  84.4 2.1 copy-done.3
  86.5 2.4 fusion.16
  89.0 1.7 dynamic-slice_bitcast_fusion.1
  91.4 3.9 collective-permute-done
  95.3 2.4 bitcast_add_fusion.1
  97.9 1.3 collective-permute-start.1
  99.1 23.3 %collective-permute-done.1 = f32[2048,128]{1,0:T(8,128)} collective-permute-done((f32[2048,128]{1,0:T(8,128)S(1)}, f32[2048,128]{1,0:T(8,128)}, u32[]{:S(2)}, u32[]{:S(2)}) %collective-permute-start.1) | collective-permute-done | bytes 1048608 | tf_op jit(solution)/shard_map/ppermute | solution.py:16
  122.4 1.3 bitcast_add_fusion.3
  123.8 1.3 collective-permute-start.2
  125.1 11.0 %collective-permute-done.2 = f32[1024,128]{1,0:T(8,128)S(1)} collective-permute-done((f32[1024,128]{1,0:T(8,128)S(1)}, f32[1024,128]{1,0:T(8,128)S(1)}, u32[]{:S(2)}, u32[]{:S(2)}) %collective-permute-start.2) | collective-permute-done | bytes 524320 | tf_op jit(solution)/shard_map/ppermute | solution.py:16
  136.4 5.5 collective-permute-done.3
  142.2 5.1 collective-permute-done.4
  147.3 1.3 collective-permute-start.5
  148.6 8.0 %collective-permute-done.5 = f32[1024,128]{1,0:T(8,128)S(1)} collective-permute-done((f32[1024,128]{1,0:T(8,128)S(1)}, f32[1024,128]{1,0:T(8,128)S(1)}, u32[]{:S(2)}, u32[]{:S(2)}) %collective-permute-start.5) | collective-permute-done | bytes 524320 | tf_op jit(solution)/shard_map/ppermute | solution.py:16
  156.7 1.3 collective-permute-start.6
  158.0 18.4 %collective-permute-done.6 = f32[2048,128]{1,0:T(8,128)} collective-permute-done((f32[2048,128]{1,0:T(8,128)S(1)}, f32[2048,128]{1,0:T(8,128)}, u32[]{:S(2)}, u32[]{:S(2)}) %collective-permute-start.6) | collective-permute-done | bytes 1048608 | tf_op jit(solution)/shard_map/ppermute | solution.py:16
  176.4 1.9 maximum_select_fusion.2
  178.3 6.1 collective-permute-start.7
  184.7 3.6 collective-permute-done.7
  188.3 23.8 %fusion.3 = f32[512,128]{1,0:T(8,128)S(1)} fusion(f32[512,8192]{1,0:T(8,128)} %param.15, s32[512]{0:T(512)S(1)} %iota_add_fusion, f32[4096,128]{1,0:T(8,128)} %collective-permute-done.7, f32[4096,128]{1,0:T(8,128)S(1)} %maximum_select_fusion.2, pred[]{:T(512)S(6)} %eq.18), kind=kOutput, calls=%fused_computation.3 | convolution fusion | flops 6453985280 | bytes 21235712 | tf_op jit(solution)/shard_map/dot_general | solution.py:125
  212.1 18.0 %fusion.5 = f32[8192,128]{1,0:T(8,128)} fusion(f32[512,128]{1,0:T(8,128)S(1)} %fusion.3, f32[8192,512]{1,0:T(8,128)} %param.17, f32[8192,128]{1,0:T(8,128)S(1)} %constant_dynamic-update-slice_fusion, f32[2,8192,128]{2,1,0:T(8,128)S(1)} %bitcast.97), kind=kOutput, calls=%fused_computation.5 | convolution fusion | flops 6444548096 | bytes 29622272 | tf_op jit(solution)/shard_map/dot_general | solution.py:129
  230.2 139.2 %all-reduce.3.cloned.1.call-done = f32[8192,128]{1,0:T(8,128)} async-done(((f32[8192,128]{1,0:T(8,128)}), f32[8192,128]{1,0:T(8,128)}) %all-reduce.3.cloned.1.call-update) | async-done | bytes 4194320 | tf_op jit(solution)/shard_map/psum | solution.py:73
  369.4 10.6 %fusion.13 = f32[256,128]{1,0:T(8,128)S(1)} fusion(f32[8192,128]{1,0:T(8,128)} %all-reduce.3.cloned.1.call-done, f32[256,8192]{1,0:T(8,128)} %param.16, s32[256]{0:T(256)S(1)} %iota_add_fusion.1), kind=kOutput, calls=%fused_computation.13 | convolution fusion | flops 3225419776 | bytes 12715008 | tf_op jit(solution)/shard_map/dot_general | solution.py:132
  380.0 17.0 %fusion.11 = f32[8192,128]{1,0:T(8,128)} fusion(f32[256,128]{1,0:T(8,128)S(1)} %fusion.13, f32[256,8192]{1,0:T(8,128)} %param.16, s32[256]{0:T(256)S(1)} %iota_add_fusion.1), kind=kOutput, calls=%fused_computation.12 | convolution fusion | flops 3225419776 | bytes 12715008 | tf_op jit(solution)/shard_map/dot_general | solution.py:133
  397.1 140.8 %all-reduce.5.cloned.1.call-done = f32[8192,128]{1,0:T(8,128)} async-done(((f32[8192,128]{1,0:T(8,128)}), f32[8192,128]{1,0:T(8,128)}) %all-reduce.5.cloned.1.call-update) | async-done | bytes 4194320 | tf_op jit(solution)/shard_map/psum | solution.py:73
  537.9 29.7 %fusion.31 = f32[512,128]{1,0:T(8,128)S(1)} fusion(f32[512,128]{1,0:T(8,128)S(1)} %fusion.3, f32[8192,128]{1,0:T(8,128)} %all-reduce.5.cloned.1.call-done, f32[8192,512]{1,0:T(8,128)} %param.17), kind=kOutput, calls=%fused_computation.41 | convolution fusion | flops 6442516480 | bytes 21495808 | tf_op jit(solution)/shard_map/dot_general | solution.py:134
  567.6 30.1 %fusion.1 = f32[8192,128]{1,0:T(8,128)S(1)} fusion(f32[512,128]{1,0:T(8,128)S(1)} %fusion.31, f32[512,8192]{1,0:T(8,128)} %param.15, s32[512]{0:T(512)S(1)} %iota_add_fusion), kind=kOutput, calls=%fused_computation.2 | convolution fusion | flops 6450839552 | bytes 21235712 | tf_op jit(solution)/shard_map/dot_general | solution.py:136
  597.8 2.2 collective-permute-start.8
  600.1 3.8 collective-permute-done.8
  604.2 1.5 collective-permute-start.9
  605.6 23.0 %collective-permute-done.9 = f32[2048,128]{1,0:T(8,128)S(1)} collective-permute-done((f32[2048,128]{1,0:T(8,128)S(1)}, f32[2048,128]{1,0:T(8,128)S(1)}, u32[]{:S(2)}, u32[]{:S(2)}) %collective-permute-start.9) | collective-permute-done | bytes 1048608 | tf_op jit(solution)/shard_map/ppermute | solution.py:16
  628.8 1.2 collective-permute-start.10
  630.0 11.0 %collective-permute-done.10 = f32[1024,128]{1,0:T(8,128)S(1)} collective-permute-done((f32[1024,128]{1,0:T(8,128)S(1)}, f32[1024,128]{1,0:T(8,128)S(1)}, u32[]{:S(2)}, u32[]{:S(2)}) %collective-permute-start.10) | collective-permute-done | bytes 524320 | tf_op jit(solution)/shard_map/ppermute | solution.py:16
  641.2 1.2 collective-permute-start.11
  642.3 4.6 collective-permute-done.11
  648.1 2.7 collective-permute-done.12
  650.9 1.2 collective-permute-start.13
  652.1 4.0 collective-permute-done.13
  656.3 1.5 collective-permute-start.14
  658.5 6.0 collective-permute-done.14
  664.7 6.6 collective-permute-start.15
  671.5 2.1 collective-permute-done.15
  674.2 3.4 fusion.35
  (72 shorter events, 11.9 us)
Async XLA Ops:
  7.2 1.1 copy-start
  7.2 362.2 %all-reduce.3.cloned.1.call-start = ((), (), s32[]{:S(2)}) async-start(), calls=%async_computation | async-start | bytes 8388608 | tf_op jit(solution)/shard_map/psum | solution.py:73
  8.3 0.7 copy-start.5
  78.8 4.5 copy-start.2
  83.3 3.2 copy-start.3
  83.3 1.1 copy-start.7
  90.7 4.7 collective-permute-start
  97.9 24.5 %collective-permute-start.1 = (f32[2048,128]{1,0:T(8,128)S(1)}, f32[2048,128]{1,0:T(8,128)}, u32[]{:S(2)}, u32[]{:S(2)}) collective-permute-start(f32[2048,128]{1,0:T(8,128)S(1)} %dynamic-slice_bitcast_fusion.3), channel_id=1, source_target_pairs={{0,2},{2,0},{1,3},{3,1},{4,6},{6,4},{5,7},{7,5},{8,10},{10,8},{9,1... | collective-permute-start | bytes 3145736 | tf_op jit(solution)/shard_map/ppermute | solution.py:16
  123.8 12.3 %collective-permute-start.2 = (f32[1024,128]{1,0:T(8,128)S(1)}, f32[1024,128]{1,0:T(8,128)S(1)}, u32[]{:S(2)}, u32[]{:S(2)}) collective-permute-start(f32[1024,128]{1,0:T(8,128)S(1)} %dynamic-slice_bitcast_fusion.5), channel_id=1, source_target_pairs={{0,4},{4,0},{8,12},{12,8},{16,20},{20,16},{24,28},{28,24},{1,5},{5... | collective-permute-start | bytes 1572872 | tf_op jit(solution)/shard_map/ppermute | solution.py:16
  136.2 5.7 collective-permute-start.3
  141.9 5.3 collective-permute-start.4
  147.3 9.3 %collective-permute-start.5 = (f32[1024,128]{1,0:T(8,128)S(1)}, f32[1024,128]{1,0:T(8,128)S(1)}, u32[]{:S(2)}, u32[]{:S(2)}) collective-permute-start(f32[1024,128]{1,0:T(8,128)S(1)} %maximum_select_fusion.6), channel_id=1, source_target_pairs={{0,4},{4,0},{8,12},{12,8},{16,20},{20,16},{24,28},{28,24},{1,5},{5... | collective-permute-start | bytes 1572872 | tf_op jit(solution)/shard_map/ppermute | solution.py:16
  156.7 19.7 %collective-permute-start.6 = (f32[2048,128]{1,0:T(8,128)S(1)}, f32[2048,128]{1,0:T(8,128)}, u32[]{:S(2)}, u32[]{:S(2)}) collective-permute-start(f32[2048,128]{1,0:T(8,128)S(1)} %maximum_select_fusion.4), channel_id=1, source_target_pairs={{0,2},{2,0},{1,3},{3,1},{4,6},{6,4},{5,7},{7,5},{8,10},{10,8},{9,1... | collective-permute-start | bytes 3145736 | tf_op jit(solution)/shard_map/ppermute | solution.py:16
  158.0 26.7 %copy-start.8 = (f32[256,128]{1,0:T(8,128)S(1)}, f32[256,128]{1,0:T(8,128)}, u32[]{:S(2)}) copy-start(f32[256,128]{1,0:T(8,128)} %param.14) | copy-start | bytes 393220
  178.3 10.0 %collective-permute-start.7 = (f32[4096,128]{1,0:T(8,128)S(1)}, f32[4096,128]{1,0:T(8,128)}, u32[]{:S(2)}, u32[]{:S(2)}) collective-permute-start(f32[4096,128]{1,0:T(8,128)S(1)} %maximum_select_fusion.2), channel_id=1, source_target_pairs={{0,1},{1,0},{2,3},{3,2},{4,5},{5,4},{6,7},{7,6},{8,9},{9,8},{10,11... | collective-permute-start | bytes 6291464 | tf_op jit(solution)/shard_map/ppermute | solution.py:16
  184.6 27.5 %slice-start.3 = ((s8[8388608]{0:T(1024)(128)(4,1)}), s8[4194304]{0:T(1024)(128)(4,1)S(1)}, s32[]{:S(2)}) async-start(s8[8388608]{0:T(1024)(128)(4,1)} %bitcast.96), calls=%async_computation.5 | async-start | bytes 8388608
  184.7 27.4 %slice-start.4 = ((s8[8388608]{0:T(1024)(128)(4,1)}), s8[4194304]{0:T(1024)(128)(4,1)S(1)}, s32[]{:S(2)}) async-start(s8[8388608]{0:T(1024)(128)(4,1)} %bitcast.96), calls=%async_computation.6 | async-start | bytes 8388608
  230.1 307.8 %all-reduce.5.cloned.1.call-start = ((), (), s32[]{:S(2)}) async-start(), calls=%async_computation.1 | async-start | bytes 8388608 | tf_op jit(solution)/shard_map/psum | solution.py:73
  597.8 6.0 collective-permute-start.8
  603.9 70.3 %slice-start = ((s8[12582912]{0:T(1024)(128)(4,1)}), s8[4194304]{0:T(1024)(128)(4,1)S(1)}, s32[]{:S(2)}) async-start(s8[12582912]{0:T(1024)(128)(4,1)} %bitcast.94), calls=%async_computation.2 | async-start | bytes 8388608
  604.2 53.6 %copy-start.4 = (f32[8192,128]{1,0:T(8,128)S(1)}, f32[8192,128]{1,0:T(8,128)}, u32[]{:S(2)}) copy-start(f32[8192,128]{1,0:T(8,128)} %all-reduce.5.cloned.1.call-done) | copy-start | bytes 12582916
  604.2 70.0 %slice-start.1 = ((s8[12582912]{0:T(1024)(128)(4,1)}), s8[4194304]{0:T(1024)(128)(4,1)S(1)}, s32[]{:S(2)}) async-start(s8[12582912]{0:T(1024)(128)(4,1)} %bitcast.94), calls=%async_computation.3 | async-start | bytes 8388608
  604.2 24.4 %collective-permute-start.9 = (f32[2048,128]{1,0:T(8,128)S(1)}, f32[2048,128]{1,0:T(8,128)S(1)}, u32[]{:S(2)}, u32[]{:S(2)}) collective-permute-start(f32[2048,128]{1,0:T(8,128)S(1)} %dynamic-slice_bitcast_fusion.2), channel_id=1, source_target_pairs={{0,2},{2,0},{1,3},{3,1},{4,6},{6,4},{5,7},{7,5},{8,10},{10,8},{9,1... | collective-permute-start | bytes 3145736 | tf_op jit(solution)/shard_map/ppermute | solution.py:16
  628.8 12.3 %collective-permute-start.10 = (f32[1024,128]{1,0:T(8,128)S(1)}, f32[1024,128]{1,0:T(8,128)S(1)}, u32[]{:S(2)}, u32[]{:S(2)}) collective-permute-start(f32[1024,128]{1,0:T(8,128)S(1)} %dynamic-slice_bitcast_fusion.4), channel_id=1, source_target_pairs={{0,4},{4,0},{8,12},{12,8},{16,20},{20,16},{24,28},{28,24},{1,5},{5... | collective-permute-start | bytes 1572872 | tf_op jit(solution)/shard_map/ppermute | solution.py:16
  641.2 5.7 collective-permute-start.11
  646.9 3.9 collective-permute-start.12
  650.9 5.3 collective-permute-start.13
  656.3 8.1 %collective-permute-start.14 = (bf16[2048,128]{1,0:T(8,128)(2,1)S(1)}, bf16[2048,128]{1,0:T(8,128)(2,1)S(1)}, u32[]{:S(2)}, u32[]{:S(2)}) collective-permute-start(bf16[2048,128]{1,0:T(8,128)(2,1)S(1)} %maximum_select_fusion.7), channel_id=1, source_target_pairs={{0,2},{2,0},{1,3},{3,1},{4,6},{6,4},{5,7},{7,5},{8,10},{10,8},{9,1... | collective-permute-start | bytes 1572872 | tf_op jit(solution)/shard_map/ppermute | solution.py:16
  664.7 9.4 %slice-start.2 = ((s8[12582912]{0:T(1024)(128)(4,1)}), s8[4194304]{0:T(1024)(128)(4,1)S(1)}, s32[]{:S(2)}) async-start(s8[12582912]{0:T(1024)(128)(4,1)} %bitcast.94), calls=%async_computation.4 | async-start | bytes 8388608
  664.7 8.8 %collective-permute-start.15 = (bf16[4096,128]{1,0:T(8,128)(2,1)S(1)}, bf16[4096,128]{1,0:T(8,128)(2,1)S(1)}, u32[]{:S(2)}, u32[]{:S(2)}) collective-permute-start(bf16[4096,128]{1,0:T(8,128)(2,1)S(1)} %maximum_select_fusion.5), channel_id=1, source_target_pairs={{0,1},{1,0},{2,3},{3,2},{4,5},{5,4},{6,7},{7,6},{8,9},{9,8},{10,11... | collective-permute-start | bytes 3145736 | tf_op jit(solution)/shard_map/ppermute | solution.py:16
  674.2 3.4 copy-start.6
  674.2 4.4 copy-start.1
Sparse Core Ops, SparseCore 0:
  230.2 139.0 all-reduce.2
  397.2 140.6 all-reduce.4
where the time goes:
time: 697 us; the launch traced here: 686 us
  waiting for transfers between devices  416 us (60%)
  matrix products  138 us (20%)
  local copies, waits for them, and re-layouts  67.7 us (10%)
  starting transfers between devices  29.1 us (4%)
  other arithmetic  20.6 us (3%)
  between operations  14.7 us (2%)
    psum x2, waiting for transfers between devices, top_total(): return lax.psum(partial_value, ('leaf', 'sep'))  280 us
    ppermute x16, waiting for transfers between devices, swapped(): return lax.ppermute(block, axis, route)  136 us
    mul x2, local copies, waits for them, and re-layouts, body(): leaf_coupling.reshape(level_total, tile_mask.shape[1], block_size, local_...  41.9 us
    dot_general x1, matrix products, body(): jnp.dot(low_factor.T, first_rows - carried, precision=PRECISE)  30.1 us
    dot_general x1, matrix products, body(): carried = jnp.dot(low_coupling.T, top_solution, precision=PRECISE)  29.7 us
    ppermute x16, starting transfers between devices, swapped(): return lax.ppermute(block, axis, route)  29 us
    dot_general x1, matrix products, body(): first_rows = jnp.dot(low_factor, first_input, precision=PRECISE)  23.8 us
    unnamed x29, local copies, waits for them, and re-layouts  21.4 us
  transfers between devices with their start and end apart: 18, of which 18 were waited for; matrix products, arithmetic and copies ran while one was open for 0% of the time, Pallas kernels for 0%

commit v1 on v0

v1 whole, which is shorter than its diff:
```python
import functools

import jax
import jax.numpy as jnp
from jax import lax
from jax.experimental import pallas as pl
from jax.experimental.pallas import tpu as pltpu
from jax.sharding import PartitionSpec as P

PRECISE = lax.Precision.HIGHEST
F32 = jnp.float32
BF16 = jnp.bfloat16
I16 = jnp.int16
AXES = ("leaf", "sep")
NEAR = 8
GROUP = 2 * NEAR
PAD = 16
VMEM = 56 << 20


def swap(block, offset):
    count = lax.axis_size("leaf") * lax.axis_size("sep")
    return lax.ppermute(block, AXES, [(at, at ^ offset) for at in range(count)])


def chunk_at(step, place, flip):
    return ((place[1] ^ step) << 1) | (place[0] ^ flip)


def encode(value):
    peak = jnp.max(jnp.abs(value), axis=0, keepdims=True)
    power = jnp.ceil(jnp.log2(jnp.maximum(peak, 1e-30)))
    scaled = jnp.floor(value * jnp.exp2(15.0 - power) + 0.5)
    code = jnp.clip(scaled, -32767.0, 32767.0).astype(jnp.int32).astype(I16)
    powers = jnp.broadcast_to(power, (PAD, value.shape[1])).astype(jnp.int32).astype(I16)
    return code, powers


def put(ref, coded):
    code, powers = coded
    rows = code.shape[0]
    ref[:rows, :] = code
    ref[rows:, :] = powers


def decode(block):
    rows = block.shape[0] - PAD
    power = block[rows:, :].astype(jnp.int32).astype(F32)[0:1, :]
    return block[:rows, :].astype(jnp.int32).astype(F32) * jnp.exp2(power - 15.0)


def halves(value):
    high = value.astype(BF16)
    return high, (value - high.astype(F32)).astype(BF16)


def dot(left, right):
    return jnp.dot(left, right, preferred_element_type=F32)


def masked(block, tiles, size):
    count, across = tiles.shape
    width = block.shape[1]
    lane = lax.broadcasted_iota(jnp.int32, (count, width), 1) // size
    spread = jnp.zeros((count, width), F32)
    for at in range(across):
        spread = jnp.where(lane == at, tiles[:, at : at + 1].astype(F32), spread)
    parts = []
    for at in range(count):
        row = jnp.broadcast_to(spread[at : at + 1, :], (16, width)).astype(BF16)
        tile = block[at * size : (at + 1) * size, :].reshape(size // 16, 16, width)
        parts.append((tile * row[None]).reshape(size, width))
    return jnp.concatenate(parts, 0)


def triangular(block, row_start, column_start):
    row = lax.broadcasted_iota(jnp.int32, block.shape, 0) + row_start
    column = lax.broadcasted_iota(jnp.int32, block.shape, 1) + column_start
    return jnp.where(row >= column, block, 0.0)


def add_rows(total, chunk, start, rhs):
    count = rhs.shape[0]
    size = total.shape[0]

    @pl.when(start // size == chunk)
    def _():
        where = pl.ds(pl.multiple_of(start % size, count), count)
        total[where, :] += rhs[...]


def emit(step, value, outs):
    own = outs[0]
    coded = encode(value)

    @pl.when(step == 0)
    def _():
        own[...] = value

    for at in range(1, NEAR):

        @pl.when(step == at)
        def _(at=at):
            put(outs[at], coded)


def call(kernel, place, grid, ins, outs, scratch, args, flops, moved):
    return pl.pallas_call(
        kernel,
        grid_spec=pltpu.PrefetchScalarGridSpec(
            num_scalar_prefetch=1,
            grid=grid,
            in_specs=ins,
            out_specs=[spec for spec, _ in outs],
            scratch_shapes=scratch,
        ),
        out_shape=[shape for _, shape in outs],
        compiler_params=pltpu.CompilerParams(vmem_limit_bytes=VMEM),
        cost_estimate=pl.CostEstimate(flops=flops, bytes_accessed=moved, transcendentals=0),
    )(place, *args)


def whole(shape):
    return pl.BlockSpec(shape, lambda *_: (0,) * len(shape))


def out_whole(shape, dtype):
    return whole(shape), jax.ShapeDtypeStruct(shape, dtype)


def leaf_value(place, chunk, level_block, tiles, rounded, rhs, total, size, start_at):
    total[...] = -dot(masked(level_block[0], tiles[0], size), rounded)
    add_rows(total, chunk, place[start_at], rhs)
    return total[...]


def leaf_send_kernel(size, place, leaf_rhs, inverse, coupling, tiles, rhs, sent, forward, rounded, total):
    step = pl.program_id(0)

    @pl.when(step == 0)
    def _():
        for at in range(leaf_rhs.shape[0] // size):
            rows = slice(at * size, (at + 1) * size)
            block = triangular(inverse[rows, :], 0, 0)
            value = jnp.dot(block, leaf_rhs[rows, :], precision=PRECISE, preferred_element_type=F32)
            forward[rows, :] = value
            rounded[rows, :] = value.astype(BF16)

    value = leaf_value(
        place, chunk_at(step, place, 1), coupling, tiles, rounded[...], rhs, total, size, 2
    )
    put(sent.at[0], encode(value))


def leaf_keep_kernel(size, place, rounded, coupling, tiles, rhs, received, *rest):
    step = pl.program_id(0)
    outs, total = rest[:NEAR], rest[NEAR]
    value = leaf_value(
        place, chunk_at(step, place, 0), coupling, tiles, rounded[...], rhs, total, size, 2
    )
    emit(step, value + decode(received[0]), outs)


def leaf_top_kernel(size, place, rounded, coupling, tiles, part):
    part[...] = dot(masked(coupling[0], tiles[0], size), rounded[...])


def sum_kernel(final, place, own, *rest):
    received, out = rest[:-1], rest[-1]
    value = own[...] if own.dtype == F32 else decode(own[...])
    for block in received:
        value = value + decode(block[...])
    if final:
        out[...] = value.astype(BF16)
    else:
        put(out, encode(value))


def summed(place, own, received, final=False):
    rows, columns = received[0].shape
    rows -= PAD
    shape = (rows, columns) if final else (rows + PAD, columns)
    return call(
        functools.partial(sum_kernel, final),
        place,
        (1,),
        [whole(own.shape)] + [whole(r.shape) for r in received],
        [out_whole(shape, BF16 if final else I16)],
        [],
        [own, *received],
        rows * columns * 8,
        rows * columns * 20,
    )[0]


def reduce_and_gather(place, outs, far, final=False):
    received = [swap(outs[at], at << 1) for at in range(1, NEAR)]
    coded = summed(place, outs[0], received, final and len(far) == 0)
    if far:
        coded = summed(place, coded, [swap(coded, offset) for offset in far], final)
    mine = [coded] + [swap(coded, at << 1) for at in range(1, NEAR)]
    return mine + [swap(block, 1) for block in mine]


def chunk_of(at, place):
    return chunk_at(at % NEAR, place, at // NEAR)


def factor_kernel(start_at, place, factor, *rest):
    blocks = rest[:GROUP]
    rows_out, columns_out, vector, wide, narrow = rest[GROUP:]
    step = pl.program_id(0)
    count, depth = factor.shape
    columns = vector.shape[1] // 2
    start = place[start_at]

    @pl.when(step == 0)
    def _():
        for at, block in enumerate(blocks):
            size = block.shape[0] - PAD
            high, low = halves(decode(block[...]))
            where = pl.ds(pl.multiple_of(chunk_of(at, place) * size, size), size)
            vector[where, :columns] = high
            vector[where, columns:] = low
        wide[...] = jnp.zeros_like(wide)
        narrow[...] = jnp.zeros_like(narrow)

    @pl.when(step * depth < start + count)
    def _():
        high, low = halves(triangular(factor[...], start, step * depth))
        where = pl.ds(pl.multiple_of(step * depth, depth), depth)
        wide[...] += dot(high, vector[where, :])
        narrow[...] += dot(low, vector[where, :columns])

    @pl.when(step == pl.num_programs(0) - 1)
    def _():
        value = wide[:, :columns] + wide[:, columns:] + narrow[...]
        rows_out[...] = value
        columns_out[...] = value.T


def factor_apply(place, factor, blocks, start_at):
    count, size = factor.shape
    columns = blocks[0].shape[1]
    depth = size // NEAR

    def at_factor(step, where):
        return (0, jnp.minimum(step, (where[start_at] + count - 1) // depth))

    return call(
        functools.partial(factor_kernel, start_at),
        place,
        (size // depth,),
        [pl.BlockSpec((count, depth), at_factor)] + [whole(b.shape) for b in blocks],
        [out_whole((count, columns), F32), out_whole((columns, count), F32)],
        [
            pltpu.VMEM((size, 2 * columns), BF16),
            pltpu.VMEM((count, 2 * columns), F32),
            pltpu.VMEM((count, columns), F32),
        ],
        [factor, *blocks],
        8 * count * size * columns,
        4 * count * size,
    )


def coupled_value(place, chunk, coupling, part, first, rhs, packed, total):
    columns = first.shape[1]

    @pl.when(pl.program_id(0) == 0)
    def _():
        high, low = halves(first[...])
        packed[:, :columns] = high
        packed[:, columns:] = low

    high, low = halves(coupling[...])
    product = dot(high, packed[...])
    total[...] = -(
        part[...] + (product[:, :columns] + product[:, columns:] + dot(low, packed[:, :columns]))
    )
    add_rows(total, chunk, place[3], rhs)
    return total[...]


def coupled_send_kernel(place, coupling, part, first, rhs, sent, packed, total):
    chunk = chunk_at(pl.program_id(0), place, 1)
    put(sent.at[0], encode(coupled_value(place, chunk, coupling, part, first, rhs, packed, total)))


def coupled_keep_kernel(place, coupling, part, first, rhs, received, *rest):
    step = pl.program_id(0)
    outs, packed, total = rest[:NEAR], rest[NEAR], rest[NEAR + 1]
    value = coupled_value(
        place, chunk_at(step, place, 0), coupling, part, first, rhs, packed, total
    )
    emit(step, value + decode(received[0]), outs)


def back_value(place, chunk, factor, vector, packed, start_at):
    columns = vector.shape[0]
    count, size = factor.shape

    @pl.when(pl.program_id(0) == 0)
    def _():
        high, low = halves(vector[...])
        packed[:columns, :] = high
        packed[columns:, :] = low

    high, low = halves(triangular(factor[...], place[start_at], chunk * size))
    product = dot(packed[...], high)
    return product[:columns, :] + product[columns:, :] + dot(packed[:columns, :], low)


def back_send_kernel(start_at, place, factor, vector, sent, packed):
    chunk = chunk_at(pl.program_id(0), place, 1)
    put(sent.at[0], encode(back_value(place, chunk, factor, vector, packed, start_at)))


def back_keep_kernel(start_at, place, factor, vector, received, *rest):
    step = pl.program_id(0)
    outs, packed = rest[:NEAR], rest[NEAR]
    value = back_value(place, chunk_at(step, place, 0), factor, vector, packed, start_at)
    emit(step, value + decode(received[0]), outs)


def back_apply(place, factor, vector, start_at):
    count, size = factor.shape
    columns = vector.shape[0]
    chunk = size // GROUP
    flops = 4 * count * size * columns
    moved = 2 * count * size
    coded = (columns + PAD, chunk)

    def specs(flip):
        return [
            pl.BlockSpec((count, chunk), lambda k, p: (0, chunk_at(k, p, flip))),
            whole(vector.shape),
        ]

    step_block = pl.BlockSpec((1, *coded), lambda k, p: (k, 0, 0))
    scratch = [pltpu.VMEM((2 * columns, count), BF16)]
    sent = call(
        functools.partial(back_send_kernel, start_at),
        place,
        (NEAR,),
        specs(1),
        [(step_block, jax.ShapeDtypeStruct((NEAR, *coded), I16))],
        scratch,
        [factor, vector],
        flops,
        moved,
    )[0]
    return call(
        functools.partial(back_keep_kernel, start_at),
        place,
        (NEAR,),
        specs(0) + [step_block],
        [out_whole((columns, chunk), F32)] + [out_whole(coded, I16)] * (NEAR - 1),
        scratch,
        [factor, vector, swap(sent, 1)],
        flops,
        moved,
    )


def carry_kernel(span, place, coupling, first, *rest):
    blocks = rest[:GROUP]
    gap, rounded, own, vector, wide, narrow = rest[GROUP:]
    step = pl.program_id(0)
    depth = coupling.shape[0]
    columns = first.shape[0]

    @pl.when(step == 0)
    def _():
        for at, block in enumerate(blocks):
            size = block.shape[1]
            high, low = halves(decode(block[...]))
            where = pl.ds(pl.multiple_of(chunk_of(at, place) * size, size), size)
            vector[:columns, where] = high
            vector[columns:, where] = low
        rounded[...] = vector[:columns, :]
        where = pl.ds(pl.multiple_of(place[3] // span * span, span), span)
        value = vector[:columns, where].astype(F32) + vector[columns:, where].astype(F32)
        own[...] = value.T
        wide[...] = jnp.zeros_like(wide)
        narrow[...] = jnp.zeros_like(narrow)

    @pl.when(step >= 0)
    def _():
        high, low = halves(coupling[...])
        where = pl.ds(pl.multiple_of(step * depth, depth), depth)
        wide[...] += dot(vector[:, where], high)
        narrow[...] += dot(vector[:columns, where], low)

    @pl.when(step == pl.num_programs(0) - 1)
    def _():
        gap[...] = first[...] - (wide[:columns, :] + wide[columns:, :] + narrow[...])


def leaf_back_top_kernel(size, place, path, coupling, tiles, out):
    @pl.when(pl.program_id(0) == 0)
    def _():
        out[...] = jnp.zeros_like(out)

    @pl.when(pl.program_id(0) >= 0)
    def _():
        out[...] += dot(path[...], masked(coupling[0], tiles[0], size))


def leaf_back_kernel(size, place, coupling, tiles, top, forward, inverse, *rest):
    blocks = rest[:GROUP]
    out, path, total = rest[GROUP:]
    step = pl.program_id(0)
    depth = coupling.shape[1]

    @pl.when(step == 0)
    def _():
        for at, block in enumerate(blocks):
            where = pl.ds(pl.multiple_of(chunk_of(at, place) * depth, depth), depth)
            path[:, where] = block[...]
        total[...] = top[...]

    @pl.when(step >= 0)
    def _():
        where = pl.ds(pl.multiple_of(step * depth, depth), depth)
        total[...] += dot(path[:, where], masked(coupling[0], tiles[0], size))

    @pl.when(step == pl.num_programs(0) - 1)
    def _():
        gap = forward[...] - total[...].T
        for at in range(gap.shape[0] // size):
            rows = slice(at * size, (at + 1) * size)
            block = triangular(inverse[rows, :], 0, 0).T
            out[rows, :] = jnp.dot(
                block, gap[rows, :], precision=PRECISE, preferred_element_type=F32
            )


def body(
    leaf_rhs,
    leaf_inverse,
    leaf_coupling,
    tile_mask,
    low_rhs,
    top_rhs,
    low_inverse,
    top_inverse,
    low_coupling,
):
    device_total = lax.axis_size("leaf") * lax.axis_size("sep")
    device = lax.axis_index("leaf") * lax.axis_size("sep") + lax.axis_index("sep")
    local_rows, columns = leaf_rhs.shape
    size = leaf_inverse.shape[1]
    sep_size = low_inverse.shape[1]
    low_count = low_inverse.shape[0]
    top_count = top_inverse.shape[0]
    chunk = sep_size // GROUP
    tiles = chunk // size
    across = local_rows // size
    low_far = list(range(GROUP, device_total // 2, GROUP))
    top_far = list(range(GROUP, device_total, GROUP))
    low_start = device % (device_total // 2) * low_count
    top_start = device * top_count
    place = jnp.stack([device % 2, device % GROUP // 2, low_start, top_start]).astype(jnp.int32)

    coded = (chunk + PAD, columns)
    step_block = pl.BlockSpec((1, *coded), lambda k, p: (k, 0, 0))
    sent_out = (step_block, jax.ShapeDtypeStruct((NEAR, *coded), I16))
    kept_out = [out_whole((chunk, columns), F32)] + [out_whole(coded, I16)] * (NEAR - 1)
    total = pltpu.VMEM((chunk, columns), F32)
    leaf_flops = 2 * sep_size * local_rows * columns
    leaf_moved = 2 * sep_size * local_rows

    def leaf_specs(level, where):
        return [
            pl.BlockSpec((1, chunk, local_rows), lambda k, p: (level, where(k, p), 0)),
            pl.BlockSpec((1, tiles, across), lambda k, p: (level, where(k, p), 0)),
        ]

    def parity(flip):
        return lambda k, p: chunk_at(k, p, flip)

    def straight(k, p):
        return k

    sent, forward_leaf, rounded_leaf = call(
        functools.partial(leaf_send_kernel, size),
        place,
        (NEAR,),
        [whole(leaf_rhs.shape), whole(leaf_inverse.shape), *leaf_specs(0, parity(1)), whole(low_rhs.shape)],
        [sent_out, out_whole(leaf_rhs.shape, F32), out_whole(leaf_rhs.shape, BF16)],
        [total],
        [leaf_rhs, leaf_inverse, leaf_coupling, tile_mask, low_rhs],
        leaf_flops // 2,
        leaf_moved // 2,
    )
    kept = call(
        functools.partial(leaf_keep_kernel, size),
        place,
        (NEAR,),
        [whole(rounded_leaf.shape), *leaf_specs(0, parity(0)), whole(low_rhs.shape), step_block],
        kept_out,
        [total],
        [rounded_leaf, leaf_coupling, tile_mask, low_rhs, swap(sent, 1)],
        leaf_flops // 2,
        leaf_moved // 2,
    )
    part = call(
        functools.partial(leaf_top_kernel, size),
        place,
        (GROUP,),
        [whole(rounded_leaf.shape), *leaf_specs(1, straight)],
        [
            (
                pl.BlockSpec((chunk, columns), lambda k, p: (k, 0)),
                jax.ShapeDtypeStruct((sep_size, columns), F32),
            )
        ],
        [],
        [rounded_leaf, leaf_coupling, tile_mask],
        leaf_flops,
        leaf_moved,
    )[0]
    first_input = reduce_and_gather(place, kept, low_far)
    first_rows, first_columns = factor_apply(place, low_inverse, first_input, 2)

    coupled_flops = 4 * sep_size * low_count * columns
    coupled_moved = 2 * sep_size * low_count

    def coupled_specs(flip):
        return [
            pl.BlockSpec((chunk, low_count), lambda k, p: (chunk_at(k, p, flip), 0)),
            pl.BlockSpec((chunk, columns), lambda k, p: (chunk_at(k, p, flip), 0)),
            whole(first_rows.shape),
            whole(top_rhs.shape),
        ]

    coupled_scratch = [pltpu.VMEM((low_count, 2 * columns), BF16), total]
    coupled_args = [low_coupling, part, first_rows, top_rhs]
    sent = call(
        coupled_send_kernel,
        place,
        (NEAR,),
        coupled_specs(1),
        [sent_out],
        coupled_scratch,
        coupled_args,
        coupled_flops,
        coupled_moved,
    )[0]
    kept = call(
        coupled_keep_kernel,
        place,
        (NEAR,),
        coupled_specs(0) + [step_block],
        kept_out,
        coupled_scratch,
        [*coupled_args, swap(sent, 1)],
        coupled_flops,
        coupled_moved,
    )
    top_input = reduce_and_gather(place, kept, top_far)
    _, forward_columns = factor_apply(place, top_inverse, top_input, 3)

    kept = back_apply(place, top_inverse, forward_columns, 3)
    solution_blocks = reduce_and_gather(place, kept, top_far)
    span = max(top_count, 128)
    depth = sep_size // NEAR
    gap, top_rounded, top_own = call(
        functools.partial(carry_kernel, span),
        place,
        (NEAR,),
        [pl.BlockSpec((depth, low_count), lambda k, p: (k, 0)), whole(first_columns.shape)]
        + [whole(b.shape) for b in solution_blocks],
        [
            out_whole((columns, low_count), F32),
            out_whole((columns, sep_size), BF16),
            out_whole((span, columns), F32),
        ],
        [
            pltpu.VMEM((2 * columns, sep_size), BF16),
            pltpu.VMEM((2 * columns, low_count), F32),
            pltpu.VMEM((columns, low_count), F32),
        ],
        [low_coupling, first_columns, *solution_blocks],
        2 * coupled_flops,
        2 * coupled_moved,
    )
    top_solution = lax.dynamic_slice_in_dim(top_own, top_start % span, top_count, 0)
    kept = back_apply(place, low_inverse, gap, 2)
    back_top = call(
        functools.partial(leaf_back_top_kernel, size),
        place,
        (GROUP,),
        [pl.BlockSpec((columns, chunk), lambda k, p: (0, k)), *leaf_specs(1, straight)],
        [out_whole((columns, local_rows), F32)],
        [],
        [top_rounded, leaf_coupling, tile_mask],
        leaf_flops,
        leaf_moved,
    )[0]
    path = reduce_and_gather(place, kept, low_far, True)
    interior = call(
        functools.partial(leaf_back_kernel, size),
        place,
        (GROUP,),
        [
            *leaf_specs(0, straight),
            whole(back_top.shape),
            whole(forward_leaf.shape),
            whole(leaf_inverse.shape),
        ]
        + [whole(b.shape) for b in path],
        [out_whole((local_rows, columns), F32)],
        [
            pltpu.VMEM((columns, sep_size), BF16),
            pltpu.VMEM((columns, local_rows), F32),
        ],
        [leaf_coupling, tile_mask, back_top, forward_leaf, leaf_inverse, *path],
        leaf_flops,
        leaf_moved,
    )[0]
    return interior, top_solution


def solution(mesh):
    return jax.shard_map(
        body,
        mesh=mesh,
        in_specs=(
            P(("leaf", "sep"), None),
            P(("leaf", "sep"), None),
            P(None, None, ("leaf", "sep")),
            P(None, None, ("leaf", "sep")),
            P(("leaf", "sep"), None),
            P(("leaf", "sep"), None),
            P(("leaf", "sep"), None),
            P(("leaf", "sep"), None),
            P(None, ("leaf", "sep")),
        ),
        out_specs=(P(("leaf", "sep"), None), P(("leaf", "sep"), None)),
        check_vma=False,
    )
```

time: 697 us -> 374 us (0.54); the launches traced: 686 us -> 370 us
  waiting for transfers between devices: 416 us -> 105 us
  Pallas kernels: 0 us -> 167 us
  matrix products: 138 us -> 0 us
  local copies, waits for them, and re-layouts: 67.7 us -> 15 us
  starting transfers between devices: 29.1 us -> 81.3 us
  other arithmetic: 20.6 us -> 0.58 us
  between operations: 14.7 us -> 1.41 us
    psum x2 -> x0, waiting for transfers between devices: 280 us -> none  [top_total(): return lax.psum(partial_value, ('leaf', 'sep'))]
    pallas_call x0 -> x20, Pallas kernels: none -> 167 us  [call(): pl.pallas_call(kernel, grid_spec=pltpu.PrefetchScalarGridSpec(num_scalar_...]
    dot_general x10 -> x0, matrix products: 138 us -> none  [the longest x1 30.1 us: body(): jnp.dot(low_factor.T, first_rows - carried, precision=PRECISE)]
    ppermute x16 -> x94, starting transfers between devices: 29 us -> 81.3 us  [swap(): return lax.ppermute(block, AXES, [(at, at ^ offset) for at in range(count)])]
    mul x2 -> x0, local copies, waits for them, and re-layouts: 41.9 us -> none  [body(): leaf_coupling.reshape(level_total, tile_mask.shape[1], block_size, local_...]
    ppermute x16 -> x94, waiting for transfers between devices: 136 us -> 105 us  [swap(): return lax.ppermute(block, AXES, [(at, at ^ offset) for at in range(count)])]
    mul x2 -> x0, other arithmetic: 9.89 us -> none  [the longest x1 9.86 us: body(): leaf_coupling.reshape(level_total, tile_mask.shape[1], block_size, local_...]
    unnamed x29 -> x190, local copies, waits for them, and re-layouts: 21.4 us -> 15 us
  transfers between devices with their start and end apart: 18 -> 94, of which waited for: 18 -> 48; matrix products, arithmetic and copies ran while one was open for 0% -> 0% of each run, Pallas kernels for 0% -> 7%
where the time goes in v1:
time: 374 us; the launch traced here: 370 us
  Pallas kernels  167 us (45%)
  waiting for transfers between devices  105 us (28%)
  starting transfers between devices  81.3 us (22%)
  local copies, waits for them, and re-layouts  15 us (4%)
    pallas_call x20, Pallas kernels, call(): pl.pallas_call(kernel, grid_spec=pltpu.PrefetchScalarGridSpec(num_scalar_...  167 us
    ppermute x94, waiting for transfers between devices, swap(): return lax.ppermute(block, AXES, [(at, at ^ offset) for at in range(count)])  105 us
    ppermute x94, starting transfers between devices, swap(): return lax.ppermute(block, AXES, [(at, at ^ offset) for at in range(count)])  81.3 us
    unnamed x190, local copies, waits for them, and re-layouts  15 us
  transfers between devices with their start and end apart: 94, of which 48 were waited for; matrix products, arithmetic and copies ran while one was open for 0% of the time, Pallas kernels for 7%

profile of v1, /device:TPU:25, one launch (start us, length us, event | category | flops | bytes accessed | tf_op | source)
XLA Modules:
  0.0 370.2 jit_solution(12014009391976893945)
XLA Ops:
  4.4 8.5 %shard_map.104 = (s16[8,528,128]{2,1,0:T(8,128)(2,1)}, f32[384,128]{1,0:T(8,128)}, bf16[384,128]{1,0:T(8,128)(2,1)}) custom-call(s32[4]{0:T(128)} %pad_add_fusion.place, f32[384,128]{1,0:T(8,128)} %leaf_rhs.1, f32[384,64]{1,0:T(8,128)} %copy.11.inverse, bf16[2,8192,384]{2,1,0:T(8,128)(2,1)} %coupling.15, s32[2,128,6]{2,1,0:T(8,128)} %copy.16.tiles, ...), custom_call_target="tpu_custom_call" | custom-call | flops 402653184 | bytes 3145728 | tf_op jit(solution)/shard_map/pallas_call | solution.py:108
  13.6 2.5 collective-permute-done.received
  17.1 8.8 %shard_map.105 = (f32[512,128]{1,0:T(8,128)}, s16[528,128]{1,0:T(8,128)(2,1)}, s16[528,128]{1,0:T(8,128)(2,1)}, s16[528,128]{1,0:T(8,128)(2,1)}, s16[528,128]{1,...) custom-call(s32[4]{0:T(128)} %pad_add_fusion.place, ...), custom_call_target="tpu_custom_call" | custom-call | flops 402653184 | bytes 3145728 | tf_op jit(solution)/shard_map/pallas_call | solution.py:108
  36.4 2.9 collective-permute-done.6.rest_5_
  39.3 3.5 collective-permute-done.7.rest_6_
  43.5 3.1 shard_map.106.rest_0_
  46.6 2.4 collective-permute-start.15
  54.0 2.5 collective-permute-done.14.rest_7_
  56.7 3.4 collective-permute-done.13.rest_6_
  67.5 13.6 %shard_map.108.part = f32[8192,128]{1,0:T(8,128)} custom-call(s32[4]{0:T(128)} %pad_add_fusion.place, bf16[384,128]{1,0:T(8,128)(2,1)} %get-tuple-element.43.rounded, bf16[2,8192,384]{2,1,0:T(8,128)(2,1)} %coupling.15, s32[2,128,6]{2,1,0:T(8,128)} %copy.16.tiles), custom_call_target="tpu_custom_call" | custom-call | flops 805306368 | bytes 6291456 | tf_op jit(solution)/shard_map/pallas_call | solution.py:108
  82.6 10.6 %shard_map.107 = (f32[512,128]{1,0:T(8,128)}, f32[128,512]{1,0:T(8,128)}) custom-call(s32[4]{0:T(128)} %pad_add_fusion.place, f32[512,8192]{1,0:T(8,128)} %factor.11, s16[528,128]{1,0:T(8,128)(2,1)} %shard_map.106.rest_0_, s16[528,128]{1,0:T(8,128)(2,1)} %copy-done.71, s16[528,128]{1,0:T(8,128)(2,1)} %copy-done.70, s16[528,128]{1,0:T(8,128)(2,1)} %copy-done.69, ...), custom_call_target="tpu_custom_call" | custom-call | flops 4294967296 | bytes 16777216 | tf_op jit(solution)/shard_map/pallas_call | solution.py:108
  93.3 10.0 %shard_map.109 = s16[8,528,128]{2,1,0:T(8,128)(2,1)} custom-call(s32[4]{0:T(128)} %pad_add_fusion.place, f32[8192,512]{1,0:T(8,128)} %coupling.13, f32[8192,128]{1,0:T(8,128)} %shard_map.108.part, f32[512,128]{1,0:T(8,128)} %get-tuple-element.54.first, f32[256,128]{1,0:T(8,128)} %rhs.7), custom_call_target="tpu_custom_call" | custom-call | flops 2147483648 | bytes 8388608 | tf_op jit(solution)/shard_map/pallas_call | solution.py:108
  103.3 2.8 collective-permute-done.23.received
  107.1 10.8 %shard_map.110 = (f32[512,128]{1,0:T(8,128)}, s16[528,128]{1,0:T(8,128)(2,1)}, s16[528,128]{1,0:T(8,128)(2,1)}, s16[528,128]{1,0:T(8,128)(2,1)}, s16[528,128]{1,...) custom-call(s32[4]{0:T(128)} %pad_add_fusion.place, ...), custom_call_target="tpu_custom_call" | custom-call | flops 2147483648 | bytes 8388608 | tf_op jit(solution)/shard_map/pallas_call | solution.py:108
  119.5 3.0 collective-permute-start.25
  122.5 2.4 collective-permute-start.28
  130.9 2.8 collective-permute-done.29.rest_5_
  133.7 3.5 collective-permute-done.30.rest_6_
  137.9 3.1 shard_map.111.own
  141.0 8.5 %collective-permute-done.31.rest_0_ = s16[528,128]{1,0:T(8,128)(2,1)S(1)} collective-permute-done((s16[528,128]{1,0:T(8,128)(2,1)}, s16[528,128]{1,0:T(8,128)(2,1)S(1)}, u32[]{:S(2)}, u32[]{:S(2)}) %collective-permute-start.31) | collective-permute-done | bytes 135200 | tf_op jit(solution)/shard_map/ppermute | solution.py:23
  150.2 2.4 shard_map.112.rest_0_
  159.4 2.4 collective-permute-done.38.rest_7_
  162.3 2.7 collective-permute-done.37.rest_6_
  174.7 10.3 %shard_map.113 = (f32[256,128]{1,0:T(8,128)}, f32[128,256]{1,0:T(8,128)}) custom-call(s32[4]{0:T(128)} %pad_add_fusion.place, f32[256,8192]{1,0:T(8,128)} %factor.9, s16[528,128]{1,0:T(8,128)(2,1)} %shard_map.112.rest_0_, s16[528,128]{1,0:T(8,128)(2,1)} %copy-done.56, s16[528,128]{1,0:T(8,128)(2,1)} %copy-done.55, s16[528,128]{1,0:T(8,128)(2,1)} %copy-done.54, ...), custom_call_target="tpu_custom_call" | custom-call | flops 2147483648 | bytes 8388608 | tf_op jit(solution)/shard_map/pallas_call | solution.py:108
  185.0 8.1 %shard_map.114 = s16[8,144,512]{2,1,0:T(8,128)(2,1)} custom-call(s32[4]{0:T(128)} %pad_add_fusion.place, f32[256,8192]{1,0:T(8,128)} %factor.9, f32[128,256]{1,0:T(8,128)} %get-tuple-element.63.vector), custom_call_target="tpu_custom_call" | custom-call | flops 1073741824 | bytes 4194304 | tf_op jit(solution)/shard_map/pallas_call | solution.py:108
  193.3 2.9 collective-permute-done.47.received
  197.2 8.5 %shard_map.115 = (f32[128,512]{1,0:T(8,128)}, s16[144,512]{1,0:T(8,128)(2,1)}, s16[144,512]{1,0:T(8,128)(2,1)}, s16[144,512]{1,0:T(8,128)(2,1)}, s16[144,512]{1,...) custom-call(s32[4]{0:T(128)} %pad_add_fusion.place, ...), custom_call_target="tpu_custom_call" | custom-call | flops 1073741824 | bytes 4194304 | tf_op jit(solution)/shard_map/pallas_call | solution.py:108
  211.6 2.4 collective-permute-start.54
  214.0 2.8 collective-permute-done.50.rest_2_
  216.9 3.5 collective-permute-done.53.rest_5_
  220.4 3.3 collective-permute-done.54.rest_6_
  224.3 3.1 shard_map.116.own
  227.5 9.4 %collective-permute-done.55.rest_0_ = s16[144,512]{1,0:T(8,128)(2,1)S(1)} collective-permute-done((s16[144,512]{1,0:T(8,128)(2,1)}, s16[144,512]{1,0:T(8,128)(2,1)S(1)}, u32[]{:S(2)}, u32[]{:S(2)}) %collective-permute-start.55) | collective-permute-done | bytes 147488 | tf_op jit(solution)/shard_map/ppermute | solution.py:23
  237.5 2.5 shard_map.117.rest_0_
  241.1 3.1 collective-permute-start.61
  249.0 4.6 %collective-permute-done.61.rest_6_ = s16[144,512]{1,0:T(8,128)(2,1)S(1)} collective-permute-done((s16[144,512]{1,0:T(8,128)(2,1)}, s16[144,512]{1,0:T(8,128)(2,1)S(1)}, u32[]{:S(2)}, u32[]{:S(2)}) %collective-permute-start.61) | collective-permute-done | bytes 147488 | tf_op jit(solution)/shard_map/ppermute | solution.py:23
  262.6 14.7 %shard_map.118 = (f32[128,512]{1,0:T(8,128)}, bf16[128,8192]{1,0:T(8,128)(2,1)}, f32[256,128]{1,0:T(8,128)}) custom-call(s32[4]{0:T(128)} %pad_add_fusion.place, f32[8192,512]{1,0:T(8,128)} %coupling.13, f32[128,512]{1,0:T(8,128)} %get-tuple-element.53.first, s16[144,512]{1,0:T(8,128)(2,1)} %shard_map.117.rest_0_, s16[144,512]{1,0:T(8,128)(2,1)} %copy-done.26, ...), custom_call_target="tpu_custom_call" | custom-call | flops 4294967296 | bytes 16777216 | tf_op jit(solution)/shard_map/pallas_call | solution.py:108
  277.3 9.5 %shard_map.120 = s16[8,144,512]{2,1,0:T(8,128)(2,1)} custom-call(s32[4]{0:T(128)} %pad_add_fusion.place, f32[512,8192]{1,0:T(8,128)} %factor.11, f32[128,512]{1,0:T(8,128)} %get-tuple-element.74.vector), custom_call_target="tpu_custom_call" | custom-call | flops 2147483648 | bytes 8388608 | tf_op jit(solution)/shard_map/pallas_call | solution.py:108
  287.0 2.8 collective-permute-done.71.received
  290.8 9.9 %shard_map.121 = (f32[128,512]{1,0:T(8,128)}, s16[144,512]{1,0:T(8,128)(2,1)}, s16[144,512]{1,0:T(8,128)(2,1)}, s16[144,512]{1,0:T(8,128)(2,1)}, s16[144,512]{1,...) custom-call(s32[4]{0:T(128)} %pad_add_fusion.place, ...), custom_call_target="tpu_custom_call" | custom-call | flops 2147483648 | bytes 8388608 | tf_op jit(solution)/shard_map/pallas_call | solution.py:108
  306.5 2.4 collective-permute-start.78
  311.4 3.3 collective-permute-done.77.rest_5_
  314.7 3.7 collective-permute-done.78.rest_6_
  319.1 2.9 shard_map.122.rest_0_
  322.0 2.4 collective-permute-start.86
  331.7 3.4 collective-permute-done.84.rest_6_
  342.4 12.7 %shard_map.119.top = f32[128,384]{1,0:T(8,128)} custom-call(s32[4]{0:T(128)} %pad_add_fusion.place, bf16[128,8192]{1,0:T(8,128)(2,1)} %get-tuple-element.72.path, bf16[2,8192,384]{2,1,0:T(8,128)(2,1)} %coupling.15, s32[2,128,6]{2,1,0:T(8,128)} %copy.16.tiles), custom_call_target="tpu_custom_call" | custom-call | flops 805306368 | bytes 6291456 | tf_op jit(solution)/shard_map/pallas_call | solution.py:108
  356.0 14.1 %shard_map.123 = f32[384,128]{1,0:T(8,128)} custom-call(s32[4]{0:T(128)} %pad_add_fusion.place, bf16[2,8192,384]{2,1,0:T(8,128)(2,1)} %coupling.15, s32[2,128,6]{2,1,0:T(8,128)} %copy.16.tiles, f32[128,384]{1,0:T(8,128)} %shard_map.119.top, f32[384,128]{1,0:T(8,128)} %get-tuple-element.73.forward, f32[384,64]{1,0:T(8,128)} %copy.11.inverse, ...), custom_call_target="tpu_custom_call" | custom-call | flops 805306368 | bytes 6291456 | tf_op jit(solution)/shard_map/pallas_call | solution.py:108
  (351 shorter events, 106.4 us)
Async XLA Ops:
  28.7 7.7 %collective-permute-start.5 = (s16[528,128]{1,0:T(8,128)(2,1)}, s16[528,128]{1,0:T(8,128)(2,1)S(1)}, u32[]{:S(2)}, u32[]{:S(2)}) collective-permute-start(s16[528,128]{1,0:T(8,128)(2,1)} %get-tuple-element.50), channel_id=1, source_target_pairs={{0,10},{1,11},{2,8},{3,9},{4,14},{5,15},{6,12},{7,13},{8,2},{9,3},... | collective-permute-start | bytes 405512 | tf_op jit(solution)/shard_map/ppermute | solution.py:23
  30.9 8.4 %collective-permute-start.6 = (s16[528,128]{1,0:T(8,128)(2,1)}, s16[528,128]{1,0:T(8,128)(2,1)S(1)}, u32[]{:S(2)}, u32[]{:S(2)}) collective-permute-start(s16[528,128]{1,0:T(8,128)(2,1)} %get-tuple-element.51), channel_id=1, source_target_pairs={{0,12},{1,13},{2,14},{3,15},{4,8},{5,9},{6,10},{7,11},{8,4},{9,5},... | collective-permute-start | bytes 405512 | tf_op jit(solution)/shard_map/ppermute | solution.py:23
  32.1 10.8 %collective-permute-start.7 = (s16[528,128]{1,0:T(8,128)(2,1)}, s16[528,128]{1,0:T(8,128)(2,1)S(1)}, u32[]{:S(2)}, u32[]{:S(2)}) collective-permute-start(s16[528,128]{1,0:T(8,128)(2,1)} %get-tuple-element.52), channel_id=1, source_target_pairs={{0,14},{1,15},{2,12},{3,13},{4,10},{5,11},{6,8},{7,9},{8,6},{9,7},... | collective-permute-start | bytes 405512 | tf_op jit(solution)/shard_map/ppermute | solution.py:23
  49.6 10.6 %collective-permute-start.13 = (s16[528,128]{1,0:T(8,128)(2,1)}, s16[528,128]{1,0:T(8,128)(2,1)S(1)}, u32[]{:S(2)}, u32[]{:S(2)}) collective-permute-start(s16[528,128]{1,0:T(8,128)(2,1)} %shard_map.106.rest_0_), channel_id=1, source_target_pairs={{0,12},{1,13},{2,14},{3,15},{4,8},{5,9},{6,10},{7,11},{8,4},{9,5},... | collective-permute-start | bytes 405512 | tf_op jit(solution)/shard_map/ppermute | solution.py:23
  51.4 10.3 %collective-permute-start.12 = (s16[528,128]{1,0:T(8,128)(2,1)}, s16[528,128]{1,0:T(8,128)(2,1)S(1)}, u32[]{:S(2)}, u32[]{:S(2)}) collective-permute-start(s16[528,128]{1,0:T(8,128)(2,1)} %shard_map.106.rest_0_), channel_id=1, source_target_pairs={{0,10},{1,11},{2,8},{3,9},{4,14},{5,15},{6,12},{7,13},{8,2},{9,3},... | collective-permute-start | bytes 405512 | tf_op jit(solution)/shard_map/ppermute | solution.py:23
  52.5 11.9 %collective-permute-start.11 = (s16[528,128]{1,0:T(8,128)(2,1)}, s16[528,128]{1,0:T(8,128)(2,1)S(1)}, u32[]{:S(2)}, u32[]{:S(2)}) collective-permute-start(s16[528,128]{1,0:T(8,128)(2,1)} %shard_map.106.rest_0_), channel_id=1, source_target_pairs={{0,8},{1,9},{2,10},{3,11},{4,12},{5,13},{6,14},{7,15},{8,0},{9,1},... | collective-permute-start | bytes 405512 | tf_op jit(solution)/shard_map/ppermute | solution.py:23
  53.8 11.4 %collective-permute-start.10 = (s16[528,128]{1,0:T(8,128)(2,1)}, s16[528,128]{1,0:T(8,128)(2,1)S(1)}, u32[]{:S(2)}, u32[]{:S(2)}) collective-permute-start(s16[528,128]{1,0:T(8,128)(2,1)} %shard_map.106.rest_0_), channel_id=1, source_target_pairs={{0,6},{1,7},{2,4},{3,5},{4,2},{5,3},{6,0},{7,1},{8,14},{9,15},{10,... | collective-permute-start | bytes 405512 | tf_op jit(solution)/shard_map/ppermute | solution.py:23
  56.5 8.9 %collective-permute-start.9 = (s16[528,128]{1,0:T(8,128)(2,1)}, s16[528,128]{1,0:T(8,128)(2,1)S(1)}, u32[]{:S(2)}, u32[]{:S(2)}) collective-permute-start(s16[528,128]{1,0:T(8,128)(2,1)} %shard_map.106.rest_0_), channel_id=1, source_target_pairs={{0,4},{1,5},{2,6},{3,7},{4,0},{5,1},{6,2},{7,3},{8,12},{9,13},{10,... | collective-permute-start | bytes 405512 | tf_op jit(solution)/shard_map/ppermute | solution.py:23
  65.2 16.0 %collective-permute-start.20 = (s16[528,128]{1,0:T(8,128)(2,1)S(1)}, s16[528,128]{1,0:T(8,128)(2,1)S(1)}, u32[]{:S(2)}, u32[]{:S(2)}) collective-permute-start(s16[528,128]{1,0:T(8,128)(2,1)S(1)} %collective-permute-done.12.rest_5_), channel_id=1, source_target_pairs={{0,1},{1,0},{2,3},{3,2},{4,5},{5,4},{6,7},{7,6},{8,9},{9,8},{10,11... | collective-permute-start | bytes 405512 | tf_op jit(solution)/shard_map/ppermute | solution.py:23
  65.4 15.8 %collective-permute-start.19 = (s16[528,128]{1,0:T(8,128)(2,1)S(1)}, s16[528,128]{1,0:T(8,128)(2,1)S(1)}, u32[]{:S(2)}, u32[]{:S(2)}) collective-permute-start(s16[528,128]{1,0:T(8,128)(2,1)S(1)} %collective-permute-done.11.rest_4_), channel_id=1, source_target_pairs={{0,1},{1,0},{2,3},{3,2},{4,5},{5,4},{6,7},{7,6},{8,9},{9,8},{10,11... | collective-permute-start | bytes 405512 | tf_op jit(solution)/shard_map/ppermute | solution.py:23
  65.8 15.4 %collective-permute-start.18 = (s16[528,128]{1,0:T(8,128)(2,1)S(1)}, s16[528,128]{1,0:T(8,128)(2,1)S(1)}, u32[]{:S(2)}, u32[]{:S(2)}) collective-permute-start(s16[528,128]{1,0:T(8,128)(2,1)S(1)} %collective-permute-done.10.rest_3_), channel_id=1, source_target_pairs={{0,1},{1,0},{2,3},{3,2},{4,5},{5,4},{6,7},{7,6},{8,9},{9,8},{10,11... | collective-permute-start | bytes 405512 | tf_op jit(solution)/shard_map/ppermute | solution.py:23
  67.0 14.2 %collective-permute-start.17 = (s16[528,128]{1,0:T(8,128)(2,1)S(1)}, s16[528,128]{1,0:T(8,128)(2,1)S(1)}, u32[]{:S(2)}, u32[]{:S(2)}) collective-permute-start(s16[528,128]{1,0:T(8,128)(2,1)S(1)} %collective-permute-done.9.rest_2_), channel_id=1, source_target_pairs={{0,1},{1,0},{2,3},{3,2},{4,5},{5,4},{6,7},{7,6},{8,9},{9,8},{10,11... | collective-permute-start | bytes 405512 | tf_op jit(solution)/shard_map/ppermute | solution.py:23
  67.1 14.2 %collective-permute-start.16 = (s16[528,128]{1,0:T(8,128)(2,1)S(1)}, s16[528,128]{1,0:T(8,128)(2,1)S(1)}, u32[]{:S(2)}, u32[]{:S(2)}) collective-permute-start(s16[528,128]{1,0:T(8,128)(2,1)S(1)} %collective-permute-done.8.rest_1_), channel_id=1, source_target_pairs={{0,1},{1,0},{2,3},{3,2},{4,5},{5,4},{6,7},{7,6},{8,9},{9,8},{10,11... | collective-permute-start | bytes 405512 | tf_op jit(solution)/shard_map/ppermute | solution.py:23
  119.5 8.8 %collective-permute-start.25 = (s16[528,128]{1,0:T(8,128)(2,1)}, s16[528,128]{1,0:T(8,128)(2,1)S(1)}, u32[]{:S(2)}, u32[]{:S(2)}) collective-permute-start(s16[528,128]{1,0:T(8,128)(2,1)} %get-tuple-element.57), channel_id=1, source_target_pairs={{0,4},{1,5},{2,6},{3,7},{4,0},{5,1},{6,2},{7,3},{8,12},{9,13},{10,... | collective-permute-start | bytes 405512 | tf_op jit(solution)/shard_map/ppermute | solution.py:23
  122.5 8.4 %collective-permute-start.28 = (s16[528,128]{1,0:T(8,128)(2,1)}, s16[528,128]{1,0:T(8,128)(2,1)S(1)}, u32[]{:S(2)}, u32[]{:S(2)}) collective-permute-start(s16[528,128]{1,0:T(8,128)(2,1)} %get-tuple-element.60), channel_id=1, source_target_pairs={{0,10},{1,11},{2,8},{3,9},{4,14},{5,15},{6,12},{7,13},{8,2},{9,3},... | collective-permute-start | bytes 405512 | tf_op jit(solution)/shard_map/ppermute | solution.py:23
  124.9 8.9 %collective-permute-start.29 = (s16[528,128]{1,0:T(8,128)(2,1)}, s16[528,128]{1,0:T(8,128)(2,1)S(1)}, u32[]{:S(2)}, u32[]{:S(2)}) collective-permute-start(s16[528,128]{1,0:T(8,128)(2,1)} %get-tuple-element.61), channel_id=1, source_target_pairs={{0,12},{1,13},{2,14},{3,15},{4,8},{5,9},{6,10},{7,11},{8,4},{9,5},... | collective-permute-start | bytes 405512 | tf_op jit(solution)/shard_map/ppermute | solution.py:23
  128.2 9.0 %collective-permute-start.30 = (s16[528,128]{1,0:T(8,128)(2,1)}, s16[528,128]{1,0:T(8,128)(2,1)S(1)}, u32[]{:S(2)}, u32[]{:S(2)}) collective-permute-start(s16[528,128]{1,0:T(8,128)(2,1)} %get-tuple-element.62), channel_id=1, source_target_pairs={{0,14},{1,15},{2,12},{3,13},{4,10},{5,11},{6,8},{7,9},{8,6},{9,7},... | collective-permute-start | bytes 405512 | tf_op jit(solution)/shard_map/ppermute | solution.py:23
  141.0 8.5 %collective-permute-start.31 = (s16[528,128]{1,0:T(8,128)(2,1)}, s16[528,128]{1,0:T(8,128)(2,1)S(1)}, u32[]{:S(2)}, u32[]{:S(2)}) collective-permute-start(s16[528,128]{1,0:T(8,128)(2,1)} %shard_map.111.own), channel_id=1, source_target_pairs={{0,16},{1,17},{2,18},{3,19},{4,20},{5,21},{6,22},{7,23},{8,24},{9,... | collective-permute-start | bytes 405512 | tf_op jit(solution)/shard_map/ppermute | solution.py:23
  154.1 10.9 %collective-permute-start.37 = (s16[528,128]{1,0:T(8,128)(2,1)}, s16[528,128]{1,0:T(8,128)(2,1)S(1)}, u32[]{:S(2)}, u32[]{:S(2)}) collective-permute-start(s16[528,128]{1,0:T(8,128)(2,1)} %shard_map.112.rest_0_), channel_id=1, source_target_pairs={{0,12},{1,13},{2,14},{3,15},{4,8},{5,9},{6,10},{7,11},{8,4},{9,5},... | collective-permute-start | bytes 405512 | tf_op jit(solution)/shard_map/ppermute | solution.py:23
  156.2 11.1 %collective-permute-start.36 = (s16[528,128]{1,0:T(8,128)(2,1)}, s16[528,128]{1,0:T(8,128)(2,1)S(1)}, u32[]{:S(2)}, u32[]{:S(2)}) collective-permute-start(s16[528,128]{1,0:T(8,128)(2,1)} %shard_map.112.rest_0_), channel_id=1, source_target_pairs={{0,10},{1,11},{2,8},{3,9},{4,14},{5,15},{6,12},{7,13},{8,2},{9,3},... | collective-permute-start | bytes 405512 | tf_op jit(solution)/shard_map/ppermute | solution.py:23
  156.8 12.9 %collective-permute-start.35 = (s16[528,128]{1,0:T(8,128)(2,1)}, s16[528,128]{1,0:T(8,128)(2,1)S(1)}, u32[]{:S(2)}, u32[]{:S(2)}) collective-permute-start(s16[528,128]{1,0:T(8,128)(2,1)} %shard_map.112.rest_0_), channel_id=1, source_target_pairs={{0,8},{1,9},{2,10},{3,11},{4,12},{5,13},{6,14},{7,15},{8,0},{9,1},... | collective-permute-start | bytes 405512 | tf_op jit(solution)/shard_map/ppermute | solution.py:23
  158.8 11.7 %collective-permute-start.34 = (s16[528,128]{1,0:T(8,128)(2,1)}, s16[528,128]{1,0:T(8,128)(2,1)S(1)}, u32[]{:S(2)}, u32[]{:S(2)}) collective-permute-start(s16[528,128]{1,0:T(8,128)(2,1)} %shard_map.112.rest_0_), channel_id=1, source_target_pairs={{0,6},{1,7},{2,4},{3,5},{4,2},{5,3},{6,0},{7,1},{8,14},{9,15},{10,... | collective-permute-start | bytes 405512 | tf_op jit(solution)/shard_map/ppermute | solution.py:23
  161.8 8.9 %collective-permute-start.33 = (s16[528,128]{1,0:T(8,128)(2,1)}, s16[528,128]{1,0:T(8,128)(2,1)S(1)}, u32[]{:S(2)}, u32[]{:S(2)}) collective-permute-start(s16[528,128]{1,0:T(8,128)(2,1)} %shard_map.112.rest_0_), channel_id=1, source_target_pairs={{0,4},{1,5},{2,6},{3,7},{4,0},{5,1},{6,2},{7,3},{8,12},{9,13},{10,... | collective-permute-start | bytes 405512 | tf_op jit(solution)/shard_map/ppermute | solution.py:23
  207.6 9.3 %collective-permute-start.50 = (s16[144,512]{1,0:T(8,128)(2,1)}, s16[144,512]{1,0:T(8,128)(2,1)S(1)}, u32[]{:S(2)}, u32[]{:S(2)}) collective-permute-start(s16[144,512]{1,0:T(8,128)(2,1)} %get-tuple-element.67), channel_id=1, source_target_pairs={{0,6},{1,7},{2,4},{3,5},{4,2},{5,3},{6,0},{7,1},{8,14},{9,15},{10,... | collective-permute-start | bytes 442376 | tf_op jit(solution)/shard_map/ppermute | solution.py:23
  208.4 8.5 %collective-permute-start.51 = (s16[144,512]{1,0:T(8,128)(2,1)}, s16[144,512]{1,0:T(8,128)(2,1)S(1)}, u32[]{:S(2)}, u32[]{:S(2)}) collective-permute-start(s16[144,512]{1,0:T(8,128)(2,1)} %get-tuple-element.68), channel_id=1, source_target_pairs={{0,8},{1,9},{2,10},{3,11},{4,12},{5,13},{6,14},{7,15},{8,0},{9,1},... | collective-permute-start | bytes 442376 | tf_op jit(solution)/shard_map/ppermute | solution.py:23
  208.4 8.5 %collective-permute-start.52 = (s16[144,512]{1,0:T(8,128)(2,1)}, s16[144,512]{1,0:T(8,128)(2,1)S(1)}, u32[]{:S(2)}, u32[]{:S(2)}) collective-permute-start(s16[144,512]{1,0:T(8,128)(2,1)} %get-tuple-element.69), channel_id=1, source_target_pairs={{0,10},{1,11},{2,8},{3,9},{4,14},{5,15},{6,12},{7,13},{8,2},{9,3},... | collective-permute-start | bytes 442376 | tf_op jit(solution)/shard_map/ppermute | solution.py:23
  211.2 9.2 %collective-permute-start.53 = (s16[144,512]{1,0:T(8,128)(2,1)}, s16[144,512]{1,0:T(8,128)(2,1)S(1)}, u32[]{:S(2)}, u32[]{:S(2)}) collective-permute-start(s16[144,512]{1,0:T(8,128)(2,1)} %get-tuple-element.70), channel_id=1, source_target_pairs={{0,12},{1,13},{2,14},{3,15},{4,8},{5,9},{6,10},{7,11},{8,4},{9,5},... | collective-permute-start | bytes 442376 | tf_op jit(solution)/shard_map/ppermute | solution.py:23
  211.6 12.0 %collective-permute-start.54 = (s16[144,512]{1,0:T(8,128)(2,1)}, s16[144,512]{1,0:T(8,128)(2,1)S(1)}, u32[]{:S(2)}, u32[]{:S(2)}) collective-permute-start(s16[144,512]{1,0:T(8,128)(2,1)} %get-tuple-element.71), channel_id=1, source_target_pairs={{0,14},{1,15},{2,12},{3,13},{4,10},{5,11},{6,8},{7,9},{8,6},{9,7},... | collective-permute-start | bytes 442376 | tf_op jit(solution)/shard_map/ppermute | solution.py:23
  227.5 9.4 %collective-permute-start.55 = (s16[144,512]{1,0:T(8,128)(2,1)}, s16[144,512]{1,0:T(8,128)(2,1)S(1)}, u32[]{:S(2)}, u32[]{:S(2)}) collective-permute-start(s16[144,512]{1,0:T(8,128)(2,1)} %shard_map.116.own), channel_id=1, source_target_pairs={{0,16},{1,17},{2,18},{3,19},{4,20},{5,21},{6,22},{7,23},{8,24},{9,... | collective-permute-start | bytes 442376 | tf_op jit(solution)/shard_map/ppermute | solution.py:23
  241.1 12.4 %collective-permute-start.61 = (s16[144,512]{1,0:T(8,128)(2,1)}, s16[144,512]{1,0:T(8,128)(2,1)S(1)}, u32[]{:S(2)}, u32[]{:S(2)}) collective-permute-start(s16[144,512]{1,0:T(8,128)(2,1)} %shard_map.117.rest_0_), channel_id=1, source_target_pairs={{0,12},{1,13},{2,14},{3,15},{4,8},{5,9},{6,10},{7,11},{8,4},{9,5},... | collective-permute-start | bytes 442376 | tf_op jit(solution)/shard_map/ppermute | solution.py:23
  244.3 11.3 %collective-permute-start.60 = (s16[144,512]{1,0:T(8,128)(2,1)}, s16[144,512]{1,0:T(8,128)(2,1)S(1)}, u32[]{:S(2)}, u32[]{:S(2)}) collective-permute-start(s16[144,512]{1,0:T(8,128)(2,1)} %shard_map.117.rest_0_), channel_id=1, source_target_pairs={{0,10},{1,11},{2,8},{3,9},{4,14},{5,15},{6,12},{7,13},{8,2},{9,3},... | collective-permute-start | bytes 442376 | tf_op jit(solution)/shard_map/ppermute | solution.py:23
  244.3 13.9 %collective-permute-start.59 = (s16[144,512]{1,0:T(8,128)(2,1)}, s16[144,512]{1,0:T(8,128)(2,1)S(1)}, u32[]{:S(2)}, u32[]{:S(2)}) collective-permute-start(s16[144,512]{1,0:T(8,128)(2,1)} %shard_map.117.rest_0_), channel_id=1, source_target_pairs={{0,8},{1,9},{2,10},{3,11},{4,12},{5,13},{6,14},{7,15},{8,0},{9,1},... | collective-permute-start | bytes 442376 | tf_op jit(solution)/shard_map/ppermute | solution.py:23
  245.9 13.1 %collective-permute-start.58 = (s16[144,512]{1,0:T(8,128)(2,1)}, s16[144,512]{1,0:T(8,128)(2,1)S(1)}, u32[]{:S(2)}, u32[]{:S(2)}) collective-permute-start(s16[144,512]{1,0:T(8,128)(2,1)} %shard_map.117.rest_0_), channel_id=1, source_target_pairs={{0,6},{1,7},{2,4},{3,5},{4,2},{5,3},{6,0},{7,1},{8,14},{9,15},{10,... | collective-permute-start | bytes 442376 | tf_op jit(solution)/shard_map/ppermute | solution.py:23
  248.6 10.5 %collective-permute-start.57 = (s16[144,512]{1,0:T(8,128)(2,1)}, s16[144,512]{1,0:T(8,128)(2,1)S(1)}, u32[]{:S(2)}, u32[]{:S(2)}) collective-permute-start(s16[144,512]{1,0:T(8,128)(2,1)} %shard_map.117.rest_0_), channel_id=1, source_target_pairs={{0,4},{1,5},{2,6},{3,7},{4,0},{5,1},{6,2},{7,3},{8,12},{9,13},{10,... | collective-permute-start | bytes 442376 | tf_op jit(solution)/shard_map/ppermute | solution.py:23
  302.7 7.9 %collective-permute-start.74 = (s16[144,512]{1,0:T(8,128)(2,1)}, s16[144,512]{1,0:T(8,128)(2,1)S(1)}, u32[]{:S(2)}, u32[]{:S(2)}) collective-permute-start(s16[144,512]{1,0:T(8,128)(2,1)} %get-tuple-element.78), channel_id=1, source_target_pairs={{0,6},{1,7},{2,4},{3,5},{4,2},{5,3},{6,0},{7,1},{8,14},{9,15},{10,... | collective-permute-start | bytes 442376 | tf_op jit(solution)/shard_map/ppermute | solution.py:23
  303.4 8.0 %collective-permute-start.76 = (s16[144,512]{1,0:T(8,128)(2,1)}, s16[144,512]{1,0:T(8,128)(2,1)S(1)}, u32[]{:S(2)}, u32[]{:S(2)}) collective-permute-start(s16[144,512]{1,0:T(8,128)(2,1)} %get-tuple-element.80), channel_id=1, source_target_pairs={{0,10},{1,11},{2,8},{3,9},{4,14},{5,15},{6,12},{7,13},{8,2},{9,3},... | collective-permute-start | bytes 442376 | tf_op jit(solution)/shard_map/ppermute | solution.py:23
  306.1 8.6 %collective-permute-start.77 = (s16[144,512]{1,0:T(8,128)(2,1)}, s16[144,512]{1,0:T(8,128)(2,1)S(1)}, u32[]{:S(2)}, u32[]{:S(2)}) collective-permute-start(s16[144,512]{1,0:T(8,128)(2,1)} %get-tuple-element.81), channel_id=1, source_target_pairs={{0,12},{1,13},{2,14},{3,15},{4,8},{5,9},{6,10},{7,11},{8,4},{9,5},... | collective-permute-start | bytes 442376 | tf_op jit(solution)/shard_map/ppermute | solution.py:23
  306.5 11.9 %collective-permute-start.78 = (s16[144,512]{1,0:T(8,128)(2,1)}, s16[144,512]{1,0:T(8,128)(2,1)S(1)}, u32[]{:S(2)}, u32[]{:S(2)}) collective-permute-start(s16[144,512]{1,0:T(8,128)(2,1)} %get-tuple-element.82), channel_id=1, source_target_pairs={{0,14},{1,15},{2,12},{3,13},{4,10},{5,11},{6,8},{7,9},{8,6},{9,7},... | collective-permute-start | bytes 442376 | tf_op jit(solution)/shard_map/ppermute | solution.py:23
  324.7 10.3 %collective-permute-start.84 = (bf16[128,512]{1,0:T(8,128)(2,1)}, bf16[128,512]{1,0:T(8,128)(2,1)S(1)}, u32[]{:S(2)}, u32[]{:S(2)}) collective-permute-start(bf16[128,512]{1,0:T(8,128)(2,1)} %shard_map.122.rest_0_), channel_id=1, source_target_pairs={{0,12},{1,13},{2,14},{3,15},{4,8},{5,9},{6,10},{7,11},{8,4},{9,5},... | collective-permute-start | bytes 393224 | tf_op jit(solution)/shard_map/ppermute | solution.py:23
  326.8 10.1 %collective-permute-start.83 = (bf16[128,512]{1,0:T(8,128)(2,1)}, bf16[128,512]{1,0:T(8,128)(2,1)S(1)}, u32[]{:S(2)}, u32[]{:S(2)}) collective-permute-start(bf16[128,512]{1,0:T(8,128)(2,1)} %shard_map.122.rest_0_), channel_id=1, source_target_pairs={{0,10},{1,11},{2,8},{3,9},{4,14},{5,15},{6,12},{7,13},{8,2},{9,3},... | collective-permute-start | bytes 393224 | tf_op jit(solution)/shard_map/ppermute | solution.py:23
  327.6 11.6 %collective-permute-start.82 = (bf16[128,512]{1,0:T(8,128)(2,1)}, bf16[128,512]{1,0:T(8,128)(2,1)S(1)}, u32[]{:S(2)}, u32[]{:S(2)}) collective-permute-start(bf16[128,512]{1,0:T(8,128)(2,1)} %shard_map.122.rest_0_), channel_id=1, source_target_pairs={{0,8},{1,9},{2,10},{3,11},{4,12},{5,13},{6,14},{7,15},{8,0},{9,1},... | collective-permute-start | bytes 393224 | tf_op jit(solution)/shard_map/ppermute | solution.py:23
  329.1 11.0 %collective-permute-start.81 = (bf16[128,512]{1,0:T(8,128)(2,1)}, bf16[128,512]{1,0:T(8,128)(2,1)S(1)}, u32[]{:S(2)}, u32[]{:S(2)}) collective-permute-start(bf16[128,512]{1,0:T(8,128)(2,1)} %shard_map.122.rest_0_), channel_id=1, source_target_pairs={{0,6},{1,7},{2,4},{3,5},{4,2},{5,3},{6,0},{7,1},{8,14},{9,15},{10,... | collective-permute-start | bytes 393224 | tf_op jit(solution)/shard_map/ppermute | solution.py:23
  331.6 8.6 %collective-permute-start.80 = (bf16[128,512]{1,0:T(8,128)(2,1)}, bf16[128,512]{1,0:T(8,128)(2,1)S(1)}, u32[]{:S(2)}, u32[]{:S(2)}) collective-permute-start(bf16[128,512]{1,0:T(8,128)(2,1)} %shard_map.122.rest_0_), channel_id=1, source_target_pairs={{0,4},{1,5},{2,6},{3,7},{4,0},{5,1},{6,2},{7,3},{8,12},{9,13},{10,... | collective-permute-start | bytes 393224 | tf_op jit(solution)/shard_map/ppermute | solution.py:23
  340.0 15.2 %collective-permute-start.91 = (bf16[128,512]{1,0:T(8,128)(2,1)S(1)}, bf16[128,512]{1,0:T(8,128)(2,1)S(1)}, u32[]{:S(2)}, u32[]{:S(2)}) collective-permute-start(bf16[128,512]{1,0:T(8,128)(2,1)S(1)} %collective-permute-done.83.rest_5_), channel_id=1, source_target_pairs={{0,1},{1,0},{2,3},{3,2},{4,5},{5,4},{6,7},{7,6},{8,9},{9,8},{10,11... | collective-permute-start | bytes 393224 | tf_op jit(solution)/shard_map/ppermute | solution.py:23
  340.3 15.0 %collective-permute-start.90 = (bf16[128,512]{1,0:T(8,128)(2,1)S(1)}, bf16[128,512]{1,0:T(8,128)(2,1)S(1)}, u32[]{:S(2)}, u32[]{:S(2)}) collective-permute-start(bf16[128,512]{1,0:T(8,128)(2,1)S(1)} %collective-permute-done.82.rest_4_), channel_id=1, source_target_pairs={{0,1},{1,0},{2,3},{3,2},{4,5},{5,4},{6,7},{7,6},{8,9},{9,8},{10,11... | collective-permute-start | bytes 393224 | tf_op jit(solution)/shard_map/ppermute | solution.py:23
  340.7 14.5 %collective-permute-start.89 = (bf16[128,512]{1,0:T(8,128)(2,1)S(1)}, bf16[128,512]{1,0:T(8,128)(2,1)S(1)}, u32[]{:S(2)}, u32[]{:S(2)}) collective-permute-start(bf16[128,512]{1,0:T(8,128)(2,1)S(1)} %collective-permute-done.81.rest_3_), channel_id=1, source_target_pairs={{0,1},{1,0},{2,3},{3,2},{4,5},{5,4},{6,7},{7,6},{8,9},{9,8},{10,11... | collective-permute-start | bytes 393224 | tf_op jit(solution)/shard_map/ppermute | solution.py:23
  341.9 13.4 %collective-permute-start.88 = (bf16[128,512]{1,0:T(8,128)(2,1)S(1)}, bf16[128,512]{1,0:T(8,128)(2,1)S(1)}, u32[]{:S(2)}, u32[]{:S(2)}) collective-permute-start(bf16[128,512]{1,0:T(8,128)(2,1)S(1)} %collective-permute-done.80.rest_2_), channel_id=1, source_target_pairs={{0,1},{1,0},{2,3},{3,2},{4,5},{5,4},{6,7},{7,6},{8,9},{9,8},{10,11... | collective-permute-start | bytes 393224 | tf_op jit(solution)/shard_map/ppermute | solution.py:23
  342.0 13.3 %collective-permute-start.87 = (bf16[128,512]{1,0:T(8,128)(2,1)S(1)}, bf16[128,512]{1,0:T(8,128)(2,1)S(1)}, u32[]{:S(2)}, u32[]{:S(2)}) collective-permute-start(bf16[128,512]{1,0:T(8,128)(2,1)S(1)} %collective-permute-done.79.rest_1_), channel_id=1, source_target_pairs={{0,1},{1,0},{2,3},{3,2},{4,5},{5,4},{6,7},{7,6},{8,9},{9,8},{10,11... | collective-permute-start | bytes 393224 | tf_op jit(solution)/shard_map/ppermute | solution.py:23
  (140 other events, 904.5 us)

commit v2 on v0

v2 whole, which is shorter than its diff:
```python
import functools

import jax
import jax.numpy as jnp
from jax import lax
from jax.experimental import pallas as pl
from jax.experimental.pallas import tpu as pltpu
from jax.sharding import PartitionSpec as P

PRECISE = lax.Precision.HIGHEST
F32 = jnp.float32
BF16 = jnp.bfloat16
I16 = jnp.int16
AXES = ("leaf", "sep")
NEAR = 8
GROUP = 2 * NEAR
PAD = 16
VMEM = 24 << 20


def swap(block, offset):
    count = lax.axis_size("leaf") * lax.axis_size("sep")
    return lax.ppermute(block, AXES, [(at, at ^ offset) for at in range(count)])


def exchange(blocks):
    count = lax.axis_size("leaf") * lax.axis_size("sep")
    groups = [
        [first + 2 * at + core for at in range(NEAR)]
        for first in range(0, count, GROUP)
        for core in range(2)
    ]
    return lax.all_to_all(blocks, AXES, 0, 0, axis_index_groups=groups)


def collect(block):
    count = lax.axis_size("leaf") * lax.axis_size("sep")
    groups = [
        [first + 2 * at + core for at in range(NEAR)]
        for first in range(0, count, GROUP)
        for core in range(2)
    ]
    return lax.all_gather(block, AXES, axis_index_groups=groups)


def encode(value):
    peak = jnp.maximum(jnp.max(jnp.abs(value), axis=0, keepdims=True), 1e-30)
    power = jnp.ceil(jnp.log2(peak))
    part = jnp.ceil(peak * jnp.exp2(14.0 - power))
    scale = 32767.0 / (part * jnp.exp2(power - 14.0))
    code = jnp.floor(value * scale + 0.5).astype(jnp.int32).astype(I16)
    row = lax.broadcasted_iota(jnp.int32, (PAD, value.shape[1]), 0)
    return code, jnp.where(row == 0, power, part).astype(jnp.int32).astype(I16)


def put(ref, coded):
    code, head = coded
    rows = code.shape[0]
    ref[:rows, :] = code
    ref[rows:, :] = head


def decode(block):
    rows = block.shape[0] - PAD
    head = block[rows:, :].astype(jnp.int32).astype(F32)
    scale = head[1:2, :] * jnp.exp2(head[0:1, :] - 14.0) * (1.0 / 32767.0)
    return block[:rows, :].astype(jnp.int32).astype(F32) * scale


def halves(value):
    high = value.astype(BF16)
    return high, (value - high.astype(F32)).astype(BF16)


def dot(left, right):
    return jnp.dot(left, right, preferred_element_type=F32)


def spread_tiles(tiles, level, width, size):
    across = tiles.shape[0]
    flags = tiles[:, level, :].astype(F32).T
    lane = lax.broadcasted_iota(jnp.int32, (flags.shape[0], width), 1) // size
    spread = jnp.zeros((flags.shape[0], width), F32)
    for at in range(across):
        spread = jnp.where(lane == at, flags[:, at : at + 1], spread)
    return spread


def masked(block, spread, chunk, size):
    width = block.shape[1]
    count = block.shape[0] // size
    flags = spread[pl.ds(pl.multiple_of(chunk * count, count), count), :]
    parts = []
    for at in range(count):
        row = jnp.broadcast_to(flags[at : at + 1, :], (16, width)).astype(BF16)
        tile = block[at * size : (at + 1) * size, :].reshape(size // 16, 16, width)
        parts.append((tile * row[None]).reshape(size, width))
    return jnp.concatenate(parts, 0)


def triangular(block, row_start, column_start):
    row = lax.broadcasted_iota(jnp.int32, block.shape, 0) + row_start
    column = lax.broadcasted_iota(jnp.int32, block.shape, 1) + column_start
    return jnp.where(row >= column, block, 0.0)


def with_rows(value, chunk, start, rhs):
    count = rhs.shape[0]
    parts = []
    for at in range(value.shape[0] // count):
        here = (start == chunk * value.shape[0] + at * count).astype(F32)
        parts.append(value[at * count : (at + 1) * count, :] + rhs[...] * here)
    return jnp.concatenate(parts, 0) if len(parts) > 1 else parts[0]


def call(kernel, place, steps, ins, outs, scratch, args, flops, moved):
    return pl.pallas_call(
        kernel,
        grid_spec=pltpu.PrefetchScalarGridSpec(
            num_scalar_prefetch=1,
            grid=(steps,),
            in_specs=ins,
            out_specs=[spec for spec, _ in outs],
            scratch_shapes=scratch,
        ),
        out_shape=[shape for _, shape in outs],
        compiler_params=pltpu.CompilerParams(vmem_limit_bytes=VMEM),
        cost_estimate=pl.CostEstimate(flops=flops, bytes_accessed=moved, transcendentals=0),
    )(place, *args)


def whole(shape):
    return pl.BlockSpec(shape, lambda *_: (0,) * len(shape))


def out_whole(shape, dtype):
    return whole(shape), jax.ShapeDtypeStruct(shape, dtype)


def in_steps(count, shape, dtype=None):
    spec = pl.BlockSpec((count, *shape), lambda k, p: (k,) + (0,) * len(shape))
    return spec if dtype is None else (spec, jax.ShapeDtypeStruct((NEAR, *shape), dtype))


def parity_of(place, flip):
    return place[0] ^ flip


def chunk_at(place, group, at, flip):
    return (pl.program_id(0) * group + at) * 2 + parity_of(place, flip)


def leaf_send_kernel(size, place, leaf_rhs, inverse_t, coupling, tiles, rhs, sent, forward, rounded, spread):
    group = coupling.shape[1]

    @pl.when(pl.program_id(0) == 0)
    def _():
        inverse = inverse_t[...].T
        for at in range(leaf_rhs.shape[0] // size):
            rows = slice(at * size, (at + 1) * size)
            block = triangular(inverse[rows, :], 0, 0)
            value = jnp.dot(block, leaf_rhs[rows, :], precision=PRECISE, preferred_element_type=F32)
            forward[rows, :] = value
            rounded[rows, :] = value.astype(BF16)
        spread[...] = spread_tiles(tiles, 0, coupling.shape[4], size)

    for at in range(group):
        chunk = chunk_at(place, group, at, 1)
        value = -dot(masked(coupling[0, at, 0], spread, chunk, size), rounded[...])
        put(sent.at[at], encode(with_rows(value, chunk, place[1], rhs)))


def leaf_keep_kernel(size, place, rounded, coupling, tiles, rhs, received, sent, spread):
    group = coupling.shape[1]

    @pl.when(pl.program_id(0) == 0)
    def _():
        spread[...] = spread_tiles(tiles, 0, coupling.shape[4], size)

    for at in range(group):
        chunk = chunk_at(place, group, at, 0)
        value = -dot(masked(coupling[0, at, 0], spread, chunk, size), rounded[...])
        put(sent.at[at], encode(with_rows(value, chunk, place[1], rhs) + decode(received[at])))


def leaf_top_kernel(size, place, rounded, coupling, tiles, part, spread):
    group, _, rows = coupling.shape[1:4]

    @pl.when(pl.program_id(0) == 0)
    def _():
        spread[...] = spread_tiles(tiles, 1, coupling.shape[4], size)

    for at in range(group):
        for core in range(2):
            chunk = (pl.program_id(0) * group + at) * 2 + core
            part[at, core] = dot(masked(coupling[0, at, core], spread, chunk, size), rounded[...])


def sum_kernel(final, place, *rest):
    blocks, out = rest[:-1], rest[-1]
    value = None
    for stack in blocks:
        for at in range(stack.shape[0]):
            term = decode(stack[at])
            value = term if value is None else value + term
    if final:
        value = value.astype(BF16)
        for at in range(out.shape[0]):
            out[at] = value
    else:
        coded = encode(value)
        for at in range(out.shape[0]):
            put(out.at[at], coded)


def summed(place, stacks, copies, final=False):
    _, rows, columns = stacks[0].shape
    shape = (copies, rows - PAD if final else rows, columns)
    return call(
        functools.partial(sum_kernel, final),
        place,
        1,
        [whole(s.shape) for s in stacks],
        [out_whole(shape, BF16 if final else I16)],
        [],
        stacks,
        rows * columns * 8,
        rows * columns * 20,
    )[0]


def reduce_and_gather(place, sent, far, direct, final=False):
    received = exchange(sent)
    copies = NEAR if direct else 1
    coded = summed(place, [received], 1 if far else copies, final and not far)
    if far:
        coded = summed(place, [coded] + [swap(coded, offset) for offset in far], copies, final)
    mine = exchange(coded) if direct else collect(coded[0])
    return mine, swap(mine, 1)


def factor_kernel(flip, start_at, group, place, *rest):
    factors, rest = rest[:group], rest[group:]
    if flip:
        blocks, before, rows_out, columns_out, wide, narrow = rest
    else:
        blocks, rows_out, wide, narrow = rest
    step = pl.program_id(0)
    count, depth = factors[0].shape
    columns = narrow.shape[1]
    start = place[start_at]

    @pl.when(step == 0)
    def _():
        wide[...] = jnp.zeros_like(wide)
        narrow[...] = jnp.zeros_like(narrow)

    for at in range(group):
        chunk = chunk_at(place, group, at, flip)

        @pl.when(chunk * depth < start + count)
        def _(at=at, chunk=chunk):
            high, low = halves(triangular(factors[at][...], start, chunk * depth))
            upper, lower = halves(decode(blocks[at]))
            wide[...] += dot(high, jnp.concatenate([upper, lower], 1))
            narrow[...] += dot(low, upper)

    @pl.when(step == pl.num_programs(0) - 1)
    def _():
        value = wide[:, :columns] + wide[:, columns:] + narrow[...]
        if flip:
            value = value + before[...]
            columns_out[...] = value.T
        rows_out[...] = value


def factor_apply(place, factor, stacks, start_at):
    count, size = factor.shape
    depth = size // GROUP
    columns = stacks[0].shape[2]
    group = 2
    result = ()
    for flip in range(2):
        outs = [out_whole((count, columns), F32)]
        if flip:
            outs.append(out_whole((columns, count), F32))
        result = call(
            functools.partial(factor_kernel, flip, start_at, group),
            place,
            NEAR // group,
            [
                pl.BlockSpec(
                    (count, depth),
                    lambda k, p, at=at, flip=flip: (0, (k * group + at) * 2 + parity_of(p, flip)),
                )
                for at in range(group)
            ]
            + [in_steps(group, stacks[0].shape[1:])]
            + [whole(r.shape) for r in result],
            outs,
            [pltpu.VMEM((count, 2 * columns), F32), pltpu.VMEM((count, columns), F32)],
            [factor] * group + [stacks[flip], *result],
            4 * count * size * columns,
            2 * count * size,
        )
    return result


def pack_rows(first, packed):
    columns = first.shape[1]

    @pl.when(pl.program_id(0) == 0)
    def _():
        high, low = halves(first[...])
        packed[:, :columns] = high
        packed[:, columns:] = low


def coupled_kernel(flip, place, coupling, part, first, rhs, *rest):
    if flip:
        sent, packed = rest
    else:
        received, sent, packed = rest
    group = coupling.shape[0]
    columns = first.shape[1]
    pack_rows(first, packed)
    for at in range(group):
        high, low = halves(coupling[at, 0])
        product = dot(high, packed[...])
        value = product[:, :columns] + product[:, columns:] + dot(low, packed[:, :columns])
        value = -(part[at, 0] + value)
        value = with_rows(value, chunk_at(place, group, at, flip), place[2], rhs)
        if not flip:
            value = value + decode(received[at])
        put(sent.at[at], encode(value))


def pack_columns(vector, packed):
    columns = vector.shape[0]

    @pl.when(pl.program_id(0) == 0)
    def _():
        high, low = halves(vector[...])
        packed[:columns, :] = high
        packed[columns:, :] = low


def back_kernel(flip, start_at, group, place, *rest):
    factors, rest = rest[:group], rest[group:]
    if flip:
        vector, sent, packed = rest
    else:
        vector, received, sent, packed = rest
    columns = vector.shape[0]
    pack_columns(vector, packed)
    for at in range(group):
        chunk = chunk_at(place, group, at, flip)
        depth = factors[at].shape[1]
        high, low = halves(triangular(factors[at][...], place[start_at], chunk * depth))
        product = dot(packed[...], high)
        value = product[:columns, :] + product[columns:, :] + dot(packed[:columns, :], low)
        if not flip:
            value = value + decode(received[at])
        put(sent.at[at], encode(value))


def back_apply(place, factor, vector, start_at):
    count, size = factor.shape
    columns = vector.shape[0]
    chunk = size // GROUP
    coded = (columns + PAD, chunk)
    group = 2
    sent = None
    for flip in (1, 0):
        sent = call(
            functools.partial(back_kernel, flip, start_at, group),
            place,
            NEAR // group,
            [
                pl.BlockSpec(
                    (count, chunk),
                    lambda k, p, at=at, flip=flip: (0, (k * group + at) * 2 + parity_of(p, flip)),
                )
                for at in range(group)
            ]
            + [whole(vector.shape)]
            + [in_steps(group, coded)] * (1 - flip),
            [in_steps(group, coded, I16)],
            [pltpu.VMEM((2 * columns, count), BF16)],
            [factor] * group + [vector] + ([] if flip else [swap(sent, 1)]),
            4 * count * size * columns,
            2 * count * size,
        )[0]
    return sent


def carry_kernel(flip, place, coupling, blocks, before, gap, rounded, wide, narrow):
    step = pl.program_id(0)
    group = coupling.shape[0]
    columns = before.shape[0]

    @pl.when(step == 0)
    def _():
        wide[...] = jnp.zeros_like(wide)
        narrow[...] = jnp.zeros_like(narrow)

    for at in range(group):

        @pl.when(step >= 0)
        def _(at=at):
            upper, lower = halves(decode(blocks[at]))
            rounded[at] = upper
            high, low = halves(coupling[at, 0])
            wide[...] += dot(jnp.concatenate([upper, lower], 0), high)
            narrow[...] += dot(upper, low)

    @pl.when(step == pl.num_programs(0) - 1)
    def _():
        gap[...] = before[...] - (wide[:columns, :] + wide[columns:, :] + narrow[...])


def own_kernel(place, mine, other, out):
    size = out.shape[0]
    here = (place[2] // size % 2 == place[0]).astype(F32)
    out[...] = (decode(mine[0]) * here + decode(other[0]) * (1.0 - here)).T


def leaf_back_top_kernel(size, place, mine, other, near_coupling, far_coupling, tiles, out, spread):
    step = pl.program_id(0)
    group = near_coupling.shape[1]

    @pl.when(step == 0)
    def _():
        spread[...] = spread_tiles(tiles, 1, near_coupling.shape[4], size)
        out[...] = jnp.zeros_like(out)

    @pl.when(step >= 0)
    def _():
        for flip, path, coupling in ((0, mine, near_coupling), (1, other, far_coupling)):
            for at in range(group):
                chunk = chunk_at(place, group, at, flip)
                out[...] += dot(path[at], masked(coupling[0, at, 0], spread, chunk, size))


def leaf_back_kernel(flip, size, place, coupling, tiles, path, before, *rest):
    if flip:
        forward, inverse_t, out, total, spread = rest
    else:
        out, total, spread = rest
    step = pl.program_id(0)
    group = coupling.shape[1]

    @pl.when(step == 0)
    def _():
        spread[...] = spread_tiles(tiles, 0, coupling.shape[4], size)
        total[...] = before[...]

    @pl.when(step >= 0)
    def _():
        for at in range(group):
            chunk = chunk_at(place, group, at, flip)
            total[...] += dot(path[at], masked(coupling[0, at, 0], spread, chunk, size))

    @pl.when(step == pl.num_programs(0) - 1)
    def _():
        if not flip:
            out[...] = total[...]
        else:
            gap = forward[...] - total[...].T
            inverse = inverse_t[...].T
            for at in range(gap.shape[0] // size):
                rows = slice(at * size, (at + 1) * size)
                block = triangular(inverse[rows, :], 0, 0).T
                out[rows, :] = jnp.dot(
                    block, gap[rows, :], precision=PRECISE, preferred_element_type=F32
                )


def body(
    leaf_rhs,
    leaf_inverse,
    leaf_coupling,
    tile_mask,
    low_rhs,
    top_rhs,
    low_inverse,
    top_inverse,
    low_coupling,
):
    device_total = lax.axis_size("leaf") * lax.axis_size("sep")
    device = lax.axis_index("leaf") * lax.axis_size("sep") + lax.axis_index("sep")
    local_rows, columns = leaf_rhs.shape
    size = leaf_inverse.shape[1]
    levels = leaf_coupling.shape[0]
    sep_size = low_inverse.shape[1]
    low_count = low_inverse.shape[0]
    top_count = top_inverse.shape[0]
    chunk = sep_size // GROUP
    low_far = list(range(GROUP, device_total // 2, GROUP))
    top_far = list(range(GROUP, device_total, GROUP))
    low_start = device % (device_total // 2) * low_count
    top_start = device * top_count
    place = jnp.stack([device % 2, low_start, top_start]).astype(jnp.int32)

    inverse_t = leaf_inverse.T
    tiles = jnp.transpose(tile_mask, (2, 0, 1))
    coupling = leaf_coupling.reshape(levels, NEAR, 2, chunk, local_rows)
    low_blocks = low_coupling.reshape(NEAR, 2, chunk, low_count)

    coded = (chunk + PAD, columns)
    back_coded = (columns + PAD, chunk)
    spread = pltpu.VMEM((sep_size // size, local_rows), F32)
    leaf_flops = 2 * sep_size * local_rows * columns
    leaf_moved = 2 * sep_size * local_rows

    def leaf_block(level, group, flip):
        return pl.BlockSpec(
            (1, group, 1, chunk, local_rows), lambda k, p: (level, k, parity_of(p, flip), 0, 0)
        )

    group = 4
    sent, forward_leaf, rounded_leaf = call(
        functools.partial(leaf_send_kernel, size),
        place,
        NEAR // group,
        [
            whole(leaf_rhs.shape),
            whole(inverse_t.shape),
            leaf_block(0, group, 1),
            whole(tiles.shape),
            whole(low_rhs.shape),
        ],
        [in_steps(group, coded, I16), out_whole(leaf_rhs.shape, F32), out_whole(leaf_rhs.shape, BF16)],
        [spread],
        [leaf_rhs, inverse_t, coupling, tiles, low_rhs],
        leaf_flops // 2,
        leaf_moved // 2,
    )
    sent = call(
        functools.partial(leaf_keep_kernel, size),
        place,
        NEAR // group,
        [
            whole(rounded_leaf.shape),
            leaf_block(0, group, 0),
            whole(tiles.shape),
            whole(low_rhs.shape),
            in_steps(group, coded),
        ],
        [in_steps(group, coded, I16)],
        [spread],
        [rounded_leaf, coupling, tiles, low_rhs, swap(sent, 1)],
        leaf_flops // 2,
        leaf_moved // 2,
    )[0]
    group = 2
    part = call(
        functools.partial(leaf_top_kernel, size),
        place,
        NEAR // group,
        [
            whole(rounded_leaf.shape),
            pl.BlockSpec((1, group, 2, chunk, local_rows), lambda k, p: (1, k, 0, 0, 0)),
            whole(tiles.shape),
        ],
        [in_steps(group, (2, chunk, columns), F32)],
        [spread],
        [rounded_leaf, coupling, tiles],
        leaf_flops,
        leaf_moved,
    )[0]
    first_input = reduce_and_gather(place, sent, low_far, False)
    first_rows, first_columns = factor_apply(place, low_inverse, first_input, 1)

    coupled_flops = 4 * sep_size * low_count * columns
    coupled_moved = 2 * sep_size * low_count
    sent = None
    for flip in (1, 0):
        sent = call(
            functools.partial(coupled_kernel, flip),
            place,
            NEAR // group,
            [
                pl.BlockSpec(
                    (group, 1, chunk, low_count),
                    lambda k, p, flip=flip: (k, parity_of(p, flip), 0, 0),
                ),
                pl.BlockSpec(
                    (group, 1, chunk, columns),
                    lambda k, p, flip=flip: (k, parity_of(p, flip), 0, 0),
                ),
                whole(first_rows.shape),
                whole(top_rhs.shape),
            ]
            + [in_steps(group, coded)] * (1 - flip),
            [in_steps(group, coded, I16)],
            [pltpu.VMEM((low_count, 2 * columns), BF16)],
            [low_blocks, part, first_rows, top_rhs] + ([] if flip else [swap(sent, 1)]),
            coupled_flops,
            coupled_moved,
        )[0]
    top_input = reduce_and_gather(place, sent, top_far, True)
    _, forward_columns = factor_apply(place, top_inverse, top_input, 2)

    sent = back_apply(place, top_inverse, forward_columns, 2)
    solution_blocks = reduce_and_gather(place, sent, top_far, True)
    gap, rounded = first_columns, []
    for flip in range(2):
        gap, near = call(
            functools.partial(carry_kernel, flip),
            place,
            NEAR // group,
            [
                pl.BlockSpec(
                    (group, 1, chunk, low_count),
                    lambda k, p, flip=flip: (k, parity_of(p, flip), 0, 0),
                ),
                in_steps(group, back_coded),
                whole(gap.shape),
            ],
            [out_whole(gap.shape, F32), in_steps(group, (columns, chunk), BF16)],
            [pltpu.VMEM((2 * columns, low_count), F32), pltpu.VMEM((columns, low_count), F32)],
            [low_blocks, solution_blocks[flip], gap],
            coupled_flops,
            coupled_moved,
        )
        rounded.append(near)
    top_own = call(
        own_kernel,
        place,
        1,
        [pl.BlockSpec((1, *back_coded), lambda k, p: (p[2] // chunk // 2, 0, 0))] * 2,
        [out_whole((chunk, columns), F32)],
        [],
        list(solution_blocks),
        chunk * columns,
        8 * chunk * columns,
    )[0]
    top_solution = lax.dynamic_slice_in_dim(top_own, top_start % chunk, top_count, 0)
    sent = back_apply(place, low_inverse, gap, 1)
    back_top = call(
        functools.partial(leaf_back_top_kernel, size),
        place,
        NEAR // group,
        [in_steps(group, (columns, chunk))] * 2
        + [leaf_block(1, group, 0), leaf_block(1, group, 1), whole(tiles.shape)],
        [out_whole((columns, local_rows), F32)],
        [spread],
        [*rounded, coupling, coupling, tiles],
        leaf_flops,
        leaf_moved,
    )[0]
    path = reduce_and_gather(place, sent, low_far, False, True)
    group = 4
    total = pltpu.VMEM((columns, local_rows), F32)
    result = back_top
    for flip in range(2):
        last = [forward_leaf, inverse_t] if flip else []
        result = call(
            functools.partial(leaf_back_kernel, flip, size),
            place,
            NEAR // group,
            [
                leaf_block(0, group, flip),
                whole(tiles.shape),
                in_steps(group, (columns, chunk)),
                whole(back_top.shape),
            ]
            + [whole(a.shape) for a in last],
            [out_whole((local_rows, columns) if flip else (columns, local_rows), F32)],
            [total, spread],
            [coupling, tiles, path[flip], result, *last],
            leaf_flops // 2,
            leaf_moved // 2,
        )[0]
    return result, top_solution


def solution(mesh):
    return jax.shard_map(
        body,
        mesh=mesh,
        in_specs=(
            P(("leaf", "sep"), None),
            P(("leaf", "sep"), None),
            P(None, None, ("leaf", "sep")),
            P(None, None, ("leaf", "sep")),
            P(("leaf", "sep"), None),
            P(("leaf", "sep"), None),
            P(("leaf", "sep"), None),
            P(("leaf", "sep"), None),
            P(None, ("leaf", "sep")),
        ),
        out_specs=(P(("leaf", "sep"), None), P(("leaf", "sep"), None)),
        check_vma=False,
    )
```

time: 697 us -> 350 us (0.50); the launches traced: 686 us -> 346 us
  waiting for transfers between devices: 416 us -> 58.9 us
  matrix products: 138 us -> 0 us
  blocking collectives: 0 us -> 136 us
  Pallas kernels: 0 us -> 73.4 us
  local copies, waits for them, and re-layouts: 67.7 us -> 46.9 us
  other arithmetic: 20.6 us -> 0.08 us
  starting transfers between devices: 29.1 us -> 16.3 us
    psum x2 -> x0, waiting for transfers between devices: 280 us -> none  [top_total(): return lax.psum(partial_value, ('leaf', 'sep'))]
    dot_general x10 -> x0, matrix products: 138 us -> none  [the longest x1 30.1 us: body(): jnp.dot(low_factor.T, first_rows - carried, precision=PRECISE)]
    all_to_all x0 -> x6, blocking collectives: none -> 111 us  [exchange(): return lax.all_to_all(blocks, AXES, 0, 0, axis_index_groups=groups)]
    ppermute x16 -> x10, waiting for transfers between devices: 136 us -> 29.2 us  [swap(): return lax.ppermute(block, AXES, [(at, at ^ offset) for at in range(count)])]
    pallas_call x0 -> x25, Pallas kernels: none -> 73.4 us  [call(): pl.pallas_call(kernel, grid_spec=pltpu.PrefetchScalarGridSpec(num_scalar_...]
    mul x2 -> x0, local copies, waits for them, and re-layouts: 41.9 us -> none  [body(): leaf_coupling.reshape(level_total, tile_mask.shape[1], block_size, local_...]
    all_gather x0 -> x1, waiting for transfers between devices: none -> 29.7 us  [collect(): return lax.all_gather(block, AXES, axis_index_groups=groups)]
    all_gather x0 -> x1, blocking collectives: none -> 25 us  [collect(): return lax.all_gather(block, AXES, axis_index_groups=groups)]
  transfers between devices with their start and end apart: 18 -> 11, of which waited for: 18 -> 7; matrix products, arithmetic and copies ran while one was open for 0% -> 0% of each run, Pallas kernels for 0% -> 6%
where the time goes in v2:
time: 350 us; the launch traced here: 346 us
  blocking collectives  136 us (39%)
  Pallas kernels  73.4 us (21%)
  waiting for transfers between devices  58.9 us (17%)
  local copies, waits for them, and re-layouts  46.9 us (13%)
  starting transfers between devices  16.3 us (5%)
  between operations  14.5 us (4%)
    all_to_all x6, blocking collectives, exchange(): return lax.all_to_all(blocks, AXES, 0, 0, axis_index_groups=groups)  111 us
    pallas_call x25, Pallas kernels, call(): pl.pallas_call(kernel, grid_spec=pltpu.PrefetchScalarGridSpec(num_scalar_...  73.4 us
    unnamed x68, local copies, waits for them, and re-layouts  46.2 us
    all_gather x1, waiting for transfers between devices, collect(): return lax.all_gather(block, AXES, axis_index_groups=groups)  29.7 us
    ppermute x10, waiting for transfers between devices, swap(): return lax.ppermute(block, AXES, [(at, at ^ offset) for at in range(count)])  29.2 us
    all_gather x1, blocking collectives, collect(): return lax.all_gather(block, AXES, axis_index_groups=groups)  25 us
    ppermute x10, starting transfers between devices, swap(): return lax.ppermute(block, AXES, [(at, at ^ offset) for at in range(count)])  16.3 us
  transfers between devices with their start and end apart: 11, of which 7 were waited for; matrix products, arithmetic and copies ran while one was open for 0% of the time, Pallas kernels for 6%

profile of v2, /device:TPU:25, one launch (start us, length us, event | category | flops | bytes accessed | tf_op | source)
XLA Modules:
  0.0 346.4 jit_solution(1962669966470757883)
XLA Ops:
  7.3 4.6 %copy-done = bf16[2,8192,384]{2,1,0:T(8,128)(2,1)S(1)} copy-done((bf16[2,8192,384]{2,1,0:T(8,128)(2,1)S(1)}, bf16[2,8192,384]{2,1,0:T(8,128)(2,1)}, u32[]{:S(2)}) %copy-start) | copy-done | bytes 12582936
  15.4 3.0 shard_map.104
  19.7 2.3 collective-permute-done.received
  22.1 4.6 %copy-done.1 = bf16[2,8192,384]{2,1,0:T(8,128)(2,1)S(1)} copy-done((bf16[2,8192,384]{2,1,0:T(8,128)(2,1)S(1)}, bf16[2,8192,384]{2,1,0:T(8,128)(2,1)}, u32[]{:S(2)}) %copy-start.1) | copy-done | bytes 12582936
  26.6 3.0 shard_map.106
  29.7 19.0 %all_to_all.30.rest_0_ = s16[8,528,128]{2,1,0:T(8,128)(2,1)S(1)} all-to-all(s16[8,528,128]{2,1,0:T(8,128)(2,1)S(1)} %shard_map.106), channel_id=1, replica_groups={{0,2,4,6,8,10,12,14},{1,3,5,7,9,11,13,15},{16,18,20,22,24,26,28,30},{17..., dimensions={0} | all-to-all | bytes 2162688 | tf_op jit(solution)/shard_map/all_to_all | solution.py:33
  48.7 1.0 shard_map.107
  49.7 25.0 %all-gather.4.rest_2_ = s16[8,528,128]{2,1,0:T(8,128)(2,1)S(1)} all-gather(s16[1,528,128]{2,1,0:T(8,128)(2,1)S(1)} %shard_map.107), channel_id=1, replica_groups={{0,2,4,6,8,10,12,14},{1,3,5,7,9,11,13,15},{16,18,20,22,24,26,28,30},{17..., dimensions={0}, use_global_device_ids=true | all-gather | bytes 1216512 | tf_op jit(solution)/shard_map/all_gather | solution.py:43
  74.8 6.5 %collective-permute-start.1 = (s16[8,528,128]{2,1,0:T(8,128)(2,1)S(1)}, s16[8,528,128]{2,1,0:T(8,128)(2,1)S(1)}, u32[]{:S(2)}, u32[]{:S(2)}) collective-permute-start(s16[8,528,128]{2,1,0:T(8,128)(2,1)S(1)} %all-gather.4.rest_2_), channel_id=1, source_target_pairs={{0,1},{1,0},{2,3},{3,2},{4,5},{5,4},{6,7},{7,6},{8,9},{9,8},{10,11... | collective-permute-start | bytes 3244040 | tf_op jit(solution)/shard_map/ppermute | solution.py:23
  81.3 4.6 %copy-done.2 = bf16[2,8192,384]{2,1,0:T(8,128)(2,1)S(1)} copy-done((bf16[2,8192,384]{2,1,0:T(8,128)(2,1)S(1)}, bf16[2,8192,384]{2,1,0:T(8,128)(2,1)}, u32[]{:S(2)}) %copy-start.2) | copy-done | bytes 12582936
  85.8 3.2 shard_map.105.part
  89.0 2.0 copy-done.8
  91.0 3.7 %shard_map.108.rest_3_ = f32[512,128]{1,0:T(8,128)S(1)} custom-call(s32[3]{0:T(128)S(1)} %pad_add_fusion.place, f32[512,8192]{1,0:T(8,128)S(1)} %bitcast.8, f32[512,8192]{1,0:T(8,128)S(1)} %bitcast.8, s16[8,528,128]{2,1,0:T(8,128)(2,1)S(1)} %all-gather.4.rest_2_), custom_call_target="tpu_custom_call" | custom-call | flops 2147483648 | bytes 8388608 | tf_op jit(solution)/shard_map/pallas_call | solution.py:117
  94.8 3.9 %shard_map.109 = (f32[512,128]{1,0:T(8,128)S(1)}, f32[128,512]{1,0:T(8,128)S(1)}) custom-call(s32[3]{0:T(128)S(1)} %pad_add_fusion.place, f32[512,8192]{1,0:T(8,128)S(1)} %bitcast.8, f32[512,8192]{1,0:T(8,128)S(1)} %bitcast.8, s16[8,528,128]{2,1,0:T(8,128)(2,1)S(1)} %collective-permute-done.1.rest_2_, f32[512,128]{1,0:T(8,128)S(1)} %shard_map.108.rest_3_), custom_call_target="tpu_custom_call" | custom-call | flops 2147483648 | bytes 8388608 | tf_op jit(solution)/shard_map/pallas_call | solution.py:117
  98.7 5.8 %copy-done.5 = f32[8192,512]{1,0:T(8,128)S(1)} copy-done((f32[8192,512]{1,0:T(8,128)S(1)}, f32[8192,512]{1,0:T(8,128)}, u32[]{:S(2)}) %copy-start.5) | copy-done | bytes 16777240
  104.5 4.9 %shard_map.110 = s16[8,528,128]{2,1,0:T(8,128)(2,1)S(1)} custom-call(s32[3]{0:T(128)S(1)} %pad_add_fusion.place, f32[8,2,512,512]{3,2,1,0:T(8,128)S(1)} %bitcast.18, f32[8,2,512,128]{3,2,1,0:T(8,128)S(1)} %copy-done.9, f32[512,128]{1,0:T(8,128)S(1)} %get-tuple-element.14.first, f32[256,128]{1,0:T(8,128)S(1)} %copy-done.17), custom_call_target="tpu_custom_call" | custom-call | flops 2147483648 | bytes 8388608 | tf_op jit(solution)/shard_map/pallas_call | solution.py:117
  109.5 2.7 collective-permute-done.2.rest_0_
  112.2 4.9 %shard_map.111 = s16[8,528,128]{2,1,0:T(8,128)(2,1)S(1)} custom-call(s32[3]{0:T(128)S(1)} %pad_add_fusion.place, f32[8,2,512,512]{3,2,1,0:T(8,128)S(1)} %bitcast.19, f32[8,2,512,128]{3,2,1,0:T(8,128)S(1)} %copy-done.9, f32[512,128]{1,0:T(8,128)S(1)} %get-tuple-element.14.first, f32[256,128]{1,0:T(8,128)S(1)} %copy-done.17, ...), custom_call_target="tpu_custom_call" | custom-call | flops 2147483648 | bytes 8388608 | tf_op jit(solution)/shard_map/pallas_call | solution.py:117
  117.1 20.2 %all_to_all.31.rest_0_ = s16[8,528,128]{2,1,0:T(8,128)(2,1)S(1)} all-to-all(s16[8,528,128]{2,1,0:T(8,128)(2,1)S(1)} %shard_map.111), channel_id=1, replica_groups={{0,2,4,6,8,10,12,14},{1,3,5,7,9,11,13,15},{16,18,20,22,24,26,28,30},{17..., dimensions={0} | all-to-all | bytes 2162688 | tf_op jit(solution)/shard_map/all_to_all | solution.py:33
  138.5 9.2 %collective-permute-done.3.rest_1_ = s16[1,528,128]{2,1,0:T(8,128)(2,1)S(1)} collective-permute-done((s16[1,528,128]{2,1,0:T(8,128)(2,1)S(1)}, s16[1,528,128]{2,1,0:T(8,128)(2,1)S(1)}, u32[]{:S(2)}, u32[]{:S(2)}) %collective-permute-start.3) | collective-permute-done | bytes 135200 | tf_op jit(solution)/shard_map/ppermute | solution.py:23
  148.5 16.5 %all_to_all.32.rest_2_ = s16[8,528,128]{2,1,0:T(8,128)(2,1)S(1)} all-to-all(s16[8,528,128]{2,1,0:T(8,128)(2,1)S(1)} %shard_map.113), channel_id=1, replica_groups={{0,2,4,6,8,10,12,14},{1,3,5,7,9,11,13,15},{16,18,20,22,24,26,28,30},{17..., dimensions={0} | all-to-all | bytes 2162688 | tf_op jit(solution)/shard_map/all_to_all | solution.py:33
  165.0 1.8 collective-permute-start.4
  166.8 3.4 copy-done.4
  170.1 2.9 shard_map.114.rest_3_
  173.1 4.0 %shard_map.115 = (f32[256,128]{1,0:T(8,128)}, f32[128,256]{1,0:T(8,128)S(1)}) custom-call(s32[3]{0:T(128)S(1)} %pad_add_fusion.place, f32[256,8192]{1,0:T(8,128)S(1)} %copy-done.4, f32[256,8192]{1,0:T(8,128)S(1)} %copy-done.4, s16[8,528,128]{2,1,0:T(8,128)(2,1)S(1)} %collective-permute-done.4.rest_2_, f32[256,128]{1,0:T(8,128)S(1)} %shard_map.114.rest_3_), custom_call_target="tpu_custom_call" | custom-call | flops 1073741824 | bytes 4194304 | tf_op jit(solution)/shard_map/pallas_call | solution.py:117
  177.1 3.1 shard_map.116
  180.3 2.8 collective-permute-done.5.rest_3_
  183.1 3.2 shard_map.117
  186.3 18.9 %all_to_all.33.rest_0_ = s16[8,144,512]{2,1,0:T(8,128)(2,1)S(1)} all-to-all(s16[8,144,512]{2,1,0:T(8,128)(2,1)S(1)} %shard_map.117), channel_id=1, replica_groups={{0,2,4,6,8,10,12,14},{1,3,5,7,9,11,13,15},{16,18,20,22,24,26,28,30},{17..., dimensions={0} | all-to-all | bytes 2359296 | tf_op jit(solution)/shard_map/all_to_all | solution.py:33
  205.2 1.1 shard_map.118.rest_0_
  206.4 9.4 %collective-permute-done.6.rest_1_ = s16[1,144,512]{2,1,0:T(8,128)(2,1)S(1)} collective-permute-done((s16[1,144,512]{2,1,0:T(8,128)(2,1)S(1)}, s16[1,144,512]{2,1,0:T(8,128)(2,1)S(1)}, u32[]{:S(2)}, u32[]{:S(2)}) %collective-permute-start.6) | collective-permute-done | bytes 147488 | tf_op jit(solution)/shard_map/ppermute | solution.py:23
  216.5 17.6 %all_to_all.34.blocks.mine = s16[8,144,512]{2,1,0:T(8,128)(2,1)S(1)} all-to-all(s16[8,144,512]{2,1,0:T(8,128)(2,1)S(1)} %shard_map.119), channel_id=1, replica_groups={{0,2,4,6,8,10,12,14},{1,3,5,7,9,11,13,15},{16,18,20,22,24,26,28,30},{17..., dimensions={0} | all-to-all | bytes 2359296 | tf_op jit(solution)/shard_map/all_to_all | solution.py:33
  234.1 1.9 collective-permute-start.7
  236.0 5.8 %copy-done.6 = f32[8192,512]{1,0:T(8,128)S(1)} copy-done((f32[8192,512]{1,0:T(8,128)S(1)}, f32[8192,512]{1,0:T(8,128)}, u32[]{:S(2)}) %copy-start.6) | copy-done | bytes 16777240
  241.7 3.7 %shard_map.120 = (f32[128,512]{1,0:T(8,128)S(1)}, bf16[8,128,512]{2,1,0:T(8,128)(2,1)S(1)}) custom-call(s32[3]{0:T(128)S(1)} %pad_add_fusion.place, f32[8,2,512,512]{3,2,1,0:T(8,128)S(1)} %bitcast.20, s16[8,144,512]{2,1,0:T(8,128)(2,1)S(1)} %all_to_all.34.blocks.mine, f32[128,512]{1,0:T(8,128)S(1)} %copy-done.21), custom_call_target="tpu_custom_call" | custom-call | flops 2147483648 | bytes 8388608 | tf_op jit(solution)/shard_map/pallas_call | solution.py:117
  245.5 6.2 %copy-done.7 = f32[8192,512]{1,0:T(8,128)S(1)} copy-done((f32[8192,512]{1,0:T(8,128)S(1)}, f32[8192,512]{1,0:T(8,128)}, u32[]{:S(2)}) %copy-start.7) | copy-done | bytes 16777240
  251.7 3.7 %shard_map.121 = (f32[128,512]{1,0:T(8,128)S(1)}, bf16[8,128,512]{2,1,0:T(8,128)(2,1)S(1)}) custom-call(s32[3]{0:T(128)S(1)} %pad_add_fusion.place, f32[8,2,512,512]{3,2,1,0:T(8,128)S(1)} %bitcast.21, s16[8,144,512]{2,1,0:T(8,128)(2,1)S(1)} %collective-permute-done.7.blocks.other, f32[128,512]{1,0:T(8,128)S(1)} %get-tuple-element.17.before), custom_call_target="tpu_custom_call" | custom-call | flops 2147483648 | bytes 8388608 | tf_op jit(solution)/shard_map/pallas_call | solution.py:117
  255.5 4.7 %shard_map.122 = s16[8,144,512]{2,1,0:T(8,128)(2,1)S(1)} custom-call(s32[3]{0:T(128)S(1)} %pad_add_fusion.place, f32[512,8192]{1,0:T(8,128)S(1)} %bitcast.8, f32[512,8192]{1,0:T(8,128)S(1)} %bitcast.8, f32[128,512]{1,0:T(8,128)S(1)} %get-tuple-element.18.rest_2_), custom_call_target="tpu_custom_call" | custom-call | flops 2147483648 | bytes 8388608 | tf_op jit(solution)/shard_map/pallas_call | solution.py:117
  260.2 2.8 collective-permute-done.8.rest_3_
  263.1 4.8 %shard_map.123 = s16[8,144,512]{2,1,0:T(8,128)(2,1)S(1)} custom-call(s32[3]{0:T(128)S(1)} %pad_add_fusion.place, f32[512,8192]{1,0:T(8,128)S(1)} %bitcast.8, f32[512,8192]{1,0:T(8,128)S(1)} %bitcast.8, f32[128,512]{1,0:T(8,128)S(1)} %get-tuple-element.18.rest_2_, s16[8,144,512]{2,1,0:T(8,128)(2,1)S(1)} %collective-permute-done.8.rest_3_), custom_call_target="tpu_custom_call" | custom-call | flops 2147483648 | bytes 8388608 | tf_op jit(solution)/shard_map/pallas_call | solution.py:117
  267.9 19.1 %all_to_all.35.rest_0_ = s16[8,144,512]{2,1,0:T(8,128)(2,1)S(1)} all-to-all(s16[8,144,512]{2,1,0:T(8,128)(2,1)S(1)} %shard_map.123), channel_id=1, replica_groups={{0,2,4,6,8,10,12,14},{1,3,5,7,9,11,13,15},{16,18,20,22,24,26,28,30},{17..., dimensions={0} | all-to-all | bytes 2359296 | tf_op jit(solution)/shard_map/all_to_all | solution.py:33
  287.0 1.5 shard_map.124
  288.5 29.7 %all-gather.3.cloned.1.call-done.path = bf16[8,128,512]{2,1,0:T(8,128)(2,1)} async-done(((bf16[1,128,512]{2,1,0:T(8,128)(2,1)}), bf16[8,128,512]{2,1,0:T(8,128)(2,1)}) %all-gather.3.cloned.1.call-update) | async-done | bytes 1048592 | tf_op jit(solution)/shard_map/all_gather | solution.py:43
  318.2 5.0 %collective-permute-start.9 = (bf16[8,128,512]{2,1,0:T(8,128)(2,1)}, bf16[8,128,512]{2,1,0:T(8,128)(2,1)}, u32[]{:S(2)}, u32[]{:S(2)}) collective-permute-start(bf16[8,128,512]{2,1,0:T(8,128)(2,1)} %all-gather.3.cloned.1.call-done.path), channel_id=1, source_target_pairs={{0,1},{1,0},{2,3},{3,2},{4,5},{5,4},{6,7},{7,6},{8,9},{9,8},{10,11... | collective-permute-start | bytes 3145736 | tf_op jit(solution)/shard_map/ppermute | solution.py:23
  324.4 4.6 %copy-done.3 = bf16[2,8192,384]{2,1,0:T(8,128)(2,1)S(1)} copy-done((bf16[2,8192,384]{2,1,0:T(8,128)(2,1)S(1)}, bf16[2,8192,384]{2,1,0:T(8,128)(2,1)}, u32[]{:S(2)}) %copy-start.3) | copy-done | bytes 12582936
  329.0 3.5 shard_map.125.before
  333.2 2.1 shard_map.126.before
  335.4 4.2 %shard_map.127 = f32[384,128]{1,0:T(8,128)} custom-call(s32[3]{0:T(128)S(1)} %pad_add_fusion.place, bf16[2,8,2,512,384]{4,3,2,1,0:T(8,128)(2,1)S(1)} %bitcast.17, s32[6,2,128]{2,1,0:T(2,128)S(1)} %bitcast.29, bf16[8,128,512]{2,1,0:T(8,128)(2,1)} %collective-permute-done.9.path, f32[128,384]{1,0:T(8,128)S(1)} %shard_map.126.before, ...), custom_call_target="tpu_custom_call" | custom-call | flops 402653184 | bytes 3145728 | tf_op jit(solution)/shard_map/pallas_call | solution.py:117
  (79 shorter events, 9.9 us)
Async XLA Ops:
  7.2 311.0 %all-gather.3.cloned.1.call-start = ((), (), s32[]{:S(2)}) async-start(), calls=%async_computation.6 | async-start | bytes 1179648 | tf_op jit(solution)/shard_map/all_gather | solution.py:43
  7.3 4.6 %copy-start = (bf16[2,8192,384]{2,1,0:T(8,128)(2,1)S(1)}, bf16[2,8192,384]{2,1,0:T(8,128)(2,1)}, u32[]{:S(2)}) copy-start(bf16[2,8192,384]{2,1,0:T(8,128)(2,1)} %param.11) | copy-start | bytes 37748740
  11.9 0.9 copy-start.13
  12.8 0.9 copy-start.18
  13.7 0.7 copy-start.22
  14.4 0.9 copy-start.26
  15.3 6.7 %copy-start.14 = (f32[512,128]{1,0:T(8,128)S(1)}, f32[512,128]{1,0:T(8,128)}, u32[]{:S(2)}) copy-start(f32[512,128]{1,0:T(8,128)} %rhs.5) | copy-start | bytes 786436
  18.4 0.7 copy-start.24
  19.1 3.0 collective-permute-start
  22.1 4.6 %copy-start.1 = (bf16[2,8192,384]{2,1,0:T(8,128)(2,1)S(1)}, bf16[2,8192,384]{2,1,0:T(8,128)(2,1)}, u32[]{:S(2)}) copy-start(bf16[2,8192,384]{2,1,0:T(8,128)(2,1)} %param.11) | copy-start | bytes 37748740
  26.6 64.3 %slice-start = ((s8[16777216]{0:T(1024)(128)(4,1)}), s8[4194304]{0:T(1024)(128)(4,1)S(1)}, s32[]{:S(2)}) async-start(s8[16777216]{0:T(1024)(128)(4,1)} %bitcast.7), calls=%async_computation.7 | async-start | bytes 8388608
  26.6 64.3 %slice-start.1 = ((s8[16777216]{0:T(1024)(128)(4,1)}), s8[4194304]{0:T(1024)(128)(4,1)S(1)}, s32[]{:S(2)}) async-start(s8[16777216]{0:T(1024)(128)(4,1)} %bitcast.7), calls=%async_computation.8 | async-start | bytes 8388608
  48.7 42.3 %slice-start.2 = ((s8[16777216]{0:T(1024)(128)(4,1)}), s8[4194304]{0:T(1024)(128)(4,1)S(1)}, s32[]{:S(2)}) async-start(s8[16777216]{0:T(1024)(128)(4,1)} %bitcast.7), calls=%async_computation.9 | async-start | bytes 8388608
  74.8 16.2 %slice-start.3 = ((s8[16777216]{0:T(1024)(128)(4,1)}), s8[4194304]{0:T(1024)(128)(4,1)S(1)}, s32[]{:S(2)}) async-start(s8[16777216]{0:T(1024)(128)(4,1)} %bitcast.7), calls=%async_computation.10 | async-start | bytes 8388608
  74.8 20.0 %collective-permute-start.1 = (s16[8,528,128]{2,1,0:T(8,128)(2,1)S(1)}, s16[8,528,128]{2,1,0:T(8,128)(2,1)S(1)}, u32[]{:S(2)}, u32[]{:S(2)}) collective-permute-start(s16[8,528,128]{2,1,0:T(8,128)(2,1)S(1)} %all-gather.4.rest_2_), channel_id=1, source_target_pairs={{0,1},{1,0},{2,3},{3,2},{4,5},{5,4},{6,7},{7,6},{8,9},{9,8},{10,11... | collective-permute-start | bytes 3244040 | tf_op jit(solution)/shard_map/ppermute | solution.py:23
  81.3 4.6 %copy-start.2 = (bf16[2,8192,384]{2,1,0:T(8,128)(2,1)S(1)}, bf16[2,8192,384]{2,1,0:T(8,128)(2,1)}, u32[]{:S(2)}) copy-start(bf16[2,8192,384]{2,1,0:T(8,128)(2,1)} %param.11) | copy-start | bytes 37748740
  89.0 2.0 copy-start.8
  94.8 3.9 %copy-start.17 = (f32[256,128]{1,0:T(8,128)S(1)}, f32[256,128]{1,0:T(8,128)}, u32[]{:S(2)}) copy-start(f32[256,128]{1,0:T(8,128)} %rhs.7) | copy-start | bytes 393220
  94.8 3.9 %copy-start.9 = (f32[8,2,512,128]{3,2,1,0:T(8,128)S(1)}, f32[8,2,512,128]{3,2,1,0:T(8,128)}, u32[]{:S(2)}) copy-start(f32[8,2,512,128]{3,2,1,0:T(8,128)} %copy-done.8) | copy-start | bytes 12582916
  98.7 10.8 %copy-start.20 = (f32[128,512]{1,0:T(8,128)}, f32[128,512]{1,0:T(8,128)S(1)}, u32[]{:S(2)}) copy-start(f32[128,512]{1,0:T(8,128)S(1)} %get-tuple-element.16.before) | copy-start | bytes 786436
  98.7 5.9 %copy-start.5 = (f32[8192,512]{1,0:T(8,128)S(1)}, f32[8192,512]{1,0:T(8,128)}, u32[]{:S(2)}) copy-start(f32[8192,512]{1,0:T(8,128)} %param.17) | copy-start | bytes 50331652
  109.4 2.8 collective-permute-start.2
  138.4 9.3 %collective-permute-start.3 = (s16[1,528,128]{2,1,0:T(8,128)(2,1)S(1)}, s16[1,528,128]{2,1,0:T(8,128)(2,1)S(1)}, u32[]{:S(2)}, u32[]{:S(2)}) collective-permute-start(s16[1,528,128]{2,1,0:T(8,128)(2,1)S(1)} %shard_map.112.rest_0_), channel_id=1, source_target_pairs={{0,16},{1,17},{2,18},{3,19},{4,20},{5,21},{6,22},{7,23},{8,24},{9,... | collective-permute-start | bytes 405512 | tf_op jit(solution)/shard_map/ppermute | solution.py:23
  165.0 8.1 %collective-permute-start.4 = (s16[8,528,128]{2,1,0:T(8,128)(2,1)S(1)}, s16[8,528,128]{2,1,0:T(8,128)(2,1)S(1)}, u32[]{:S(2)}, u32[]{:S(2)}) collective-permute-start(s16[8,528,128]{2,1,0:T(8,128)(2,1)S(1)} %all_to_all.32.rest_2_), channel_id=1, source_target_pairs={{0,1},{1,0},{2,3},{3,2},{4,5},{5,4},{6,7},{7,6},{8,9},{9,8},{10,11... | collective-permute-start | bytes 3244040 | tf_op jit(solution)/shard_map/ppermute | solution.py:23
  166.8 3.4 copy-start.4
  180.2 2.9 collective-permute-start.5
  206.3 9.4 %collective-permute-start.6 = (s16[1,144,512]{2,1,0:T(8,128)(2,1)S(1)}, s16[1,144,512]{2,1,0:T(8,128)(2,1)S(1)}, u32[]{:S(2)}, u32[]{:S(2)}) collective-permute-start(s16[1,144,512]{2,1,0:T(8,128)(2,1)S(1)} %shard_map.118.rest_0_), channel_id=1, source_target_pairs={{0,16},{1,17},{2,18},{3,19},{4,20},{5,21},{6,22},{7,23},{8,24},{9,... | collective-permute-start | bytes 442376 | tf_op jit(solution)/shard_map/ppermute | solution.py:23
  216.5 19.5 %copy-start.21 = (f32[128,512]{1,0:T(8,128)S(1)}, f32[128,512]{1,0:T(8,128)}, u32[]{:S(2)}) copy-start(f32[128,512]{1,0:T(8,128)} %copy-done.20) | copy-start | bytes 786436
  234.1 11.4 %collective-permute-start.7 = (s16[8,144,512]{2,1,0:T(8,128)(2,1)S(1)}, s16[8,144,512]{2,1,0:T(8,128)(2,1)S(1)}, u32[]{:S(2)}, u32[]{:S(2)}) collective-permute-start(s16[8,144,512]{2,1,0:T(8,128)(2,1)S(1)} %all_to_all.34.blocks.mine), channel_id=1, source_target_pairs={{0,1},{1,0},{2,3},{3,2},{4,5},{5,4},{6,7},{7,6},{8,9},{9,8},{10,11... | collective-permute-start | bytes 3538952 | tf_op jit(solution)/shard_map/ppermute | solution.py:23
  236.0 5.8 %copy-start.6 = (f32[8192,512]{1,0:T(8,128)S(1)}, f32[8192,512]{1,0:T(8,128)}, u32[]{:S(2)}) copy-start(f32[8192,512]{1,0:T(8,128)} %param.17) | copy-start | bytes 50331652
  245.5 10.0 %copy-start.10 = (s16[8,144,512]{2,1,0:T(8,128)(2,1)}, s16[8,144,512]{2,1,0:T(8,128)(2,1)S(1)}, u32[]{:S(2)}) copy-start(s16[8,144,512]{2,1,0:T(8,128)(2,1)S(1)} %collective-permute-done.7.blocks.other) | copy-start | bytes 3538948
  245.5 6.2 %copy-start.7 = (f32[8192,512]{1,0:T(8,128)S(1)}, f32[8192,512]{1,0:T(8,128)}, u32[]{:S(2)}) copy-start(f32[8192,512]{1,0:T(8,128)} %param.17) | copy-start | bytes 50331652
  255.5 4.7 %copy-start.15 = (bf16[8,128,512]{2,1,0:T(8,128)(2,1)}, bf16[8,128,512]{2,1,0:T(8,128)(2,1)S(1)}, u32[]{:S(2)}) copy-start(bf16[8,128,512]{2,1,0:T(8,128)(2,1)S(1)} %get-tuple-element.20.other) | copy-start | bytes 3145732
  260.2 2.9 collective-permute-start.8
  287.0 36.2 %copy-start.11 = (s16[8,144,512]{2,1,0:T(8,128)(2,1)S(1)}, s16[8,144,512]{2,1,0:T(8,128)(2,1)}, u32[]{:S(2)}) copy-start(s16[8,144,512]{2,1,0:T(8,128)(2,1)} %copy-done.10) | copy-start | bytes 3538948
  318.2 17.1 %collective-permute-start.9 = (bf16[8,128,512]{2,1,0:T(8,128)(2,1)}, bf16[8,128,512]{2,1,0:T(8,128)(2,1)}, u32[]{:S(2)}, u32[]{:S(2)}) collective-permute-start(bf16[8,128,512]{2,1,0:T(8,128)(2,1)} %all-gather.3.cloned.1.call-done.path), channel_id=1, source_target_pairs={{0,1},{1,0},{2,3},{3,2},{4,5},{5,4},{6,7},{7,6},{8,9},{9,8},{10,11... | collective-permute-start | bytes 3145736 | tf_op jit(solution)/shard_map/ppermute | solution.py:23
  323.2 1.2 copy-start.16
  323.2 1.2 copy-start.23
  324.4 4.6 %copy-start.3 = (bf16[2,8192,384]{2,1,0:T(8,128)(2,1)S(1)}, bf16[2,8192,384]{2,1,0:T(8,128)(2,1)}, u32[]{:S(2)}) copy-start(bf16[2,8192,384]{2,1,0:T(8,128)(2,1)} %param.11) | copy-start | bytes 37748740
  329.0 4.1 %copy-start.12 = (bf16[8,128,512]{2,1,0:T(8,128)(2,1)S(1)}, bf16[8,128,512]{2,1,0:T(8,128)(2,1)}, u32[]{:S(2)}) copy-start(bf16[8,128,512]{2,1,0:T(8,128)(2,1)} %all-gather.3.cloned.1.call-done.path) | copy-start | bytes 3145732
  329.0 6.3 %slice-start.4 = ((s8[12582912]{0:T(1024)(128)(4,1)}), s8[4194304]{0:T(1024)(128)(4,1)S(1)}, s32[]{:S(2)}) async-start(s8[12582912]{0:T(1024)(128)(4,1)} %bitcast.15), calls=%async_computation.11 | async-start | bytes 8388608
  329.0 6.3 %slice-start.5 = ((s8[12582912]{0:T(1024)(128)(4,1)}), s8[4194304]{0:T(1024)(128)(4,1)S(1)}, s32[]{:S(2)}) async-start(s8[12582912]{0:T(1024)(128)(4,1)} %bitcast.15), calls=%async_computation.12 | async-start | bytes 8388608
  333.2 2.2 slice-start.6
  333.2 2.2 copy-start.19
  333.2 2.2 copy-start.25
Sparse Core Ops, SparseCore 0:
  288.6 29.4 all-gather.2
